TPU v7x, 128 devices: a whole 4x4x4 slice. The times are simulated.
128 devices in a mesh: dp: 32 (over x, y, core), mp: 4 (over z).
Axes of the slice: x: 4, y: 4, z: 4, core: 2. Of those that a mesh axis runs over, the one named last changes fastest.
Arguments:
- qkv: bfloat16 [24576, 3, 3072], P('dp', None, 'mp'), may hold values from -128 to 128, as said below
- segment_ids: int32 [24576], P('dp'), may hold values from -1 to 191, as said below
- block_dest: int32 [192], replicated, may hold values from 0 to 191, as said below
- q_gain: float32 [3072], P('mp'), may hold values from 0.5 to 5.2, as said below
- k_gain: float32 [3072], P('mp'), may hold values from 0.5 to 5.2, as said below
- out_weight: bfloat16 [3072, 3072], P(None, 'mp'), may hold values from -0.5 to 0.5
- cotangent: bfloat16 [24576, 3072], P(('dp', 'mp')), may hold values from -24 to 24
Outputs:
- attn_out: bfloat16 [24576, 3072], P(('dp', 'mp'))
- qkv_grad: bfloat16 [24576, 3, 3072], P('dp', None, 'mp')
- w_grad: float32 [3072, 3072], P('dp', 'mp')
Inputs may be any that keep to these rules, and one draw needn't show every extreme that they name: `block_dest`: A permutation of the 192 block positions; position p lies on dp index p // 6. No dp index sends two blocks to the same dp index, and every image's blocks take consecutive positions of one dp index. `segment_ids`: each block belongs to one image; an image's blocks are full except its last, which holds 4 to 127 real rows followed by padding rows (-1). `qkv`: entries of the query and key parts have row and column scales of their own; values of order one. `q_gain`: Positive. `k_gain`: Positive.
All inputs are finite; a program needn't handle non-finite values.
Results may differ from a plain program's by a relative error of at most 0.02.
The roundings to bfloat16 on the way count: a program that leaves them out, or rounds other values in their place, can miss the bound.
Values may be sent and summed in bfloat16 or wider, within the bound.
No kernel may reach another device: no remote copies, remote signals or barrier semaphores. Data moves between devices by JAX's collectives and lax.ppermute only.
A program may use at most 192 MiB of HBM per device.

v0:
```python
import math

import jax
import jax.numpy as jnp
from jax import lax
from jax.sharding import PartitionSpec as P

HD = 128
BLK = 128


NORM_EPS = 1e-06
MASKED_SCORE = -1e30


def dot_first(left, right):
    return lax.dot_general(
        left, right, (((0,), (0,)), ((), ())), preferred_element_type=jnp.float32
    )


def dot_last(left, right):
    return lax.dot_general(
        left, right, (((1,), (1,)), ((), ())), preferred_element_type=jnp.float32
    )


def layer_norm(inputs, norm_gain):
    values = inputs.astype(jnp.float32)
    centred = values - jnp.mean(values, axis=1, keepdims=True)
    inv_scale = lax.rsqrt(jnp.mean(centred * centred, axis=1, keepdims=True) + NORM_EPS)
    normed = centred * inv_scale
    return (normed, inv_scale, (normed * norm_gain[None, :]).astype(jnp.bfloat16))


def norm_backward(upstream, normed, inv_scale, norm_gain):
    scaled = upstream * norm_gain[None, :]
    centred = scaled - jnp.mean(scaled, axis=1, keepdims=True)
    projection_term = normed * jnp.mean(scaled * normed, axis=1, keepdims=True)
    return (inv_scale * (centred - projection_term)).astype(jnp.bfloat16)


def head_pass(queries, key_rows, value_rows, q_scale, k_scale, segments, head_grad):
    factor = 1.0 / math.sqrt(queries.shape[1])
    q_normed, q_inv, q_hat = layer_norm(queries, q_scale)
    k_normed, k_inv, k_hat = layer_norm(key_rows, k_scale)
    scores = dot_last(q_hat, k_hat) * factor
    allowed = (segments[:, None] == segments[None, :]) & (segments[None, :] >= 0)
    masked = jnp.where(allowed, scores, MASKED_SCORE)
    row_top = jnp.max(masked, axis=1, keepdims=True)
    weights = jnp.exp(masked - row_top) * allowed.astype(jnp.float32)
    totals = jnp.maximum(jnp.sum(weights, axis=1, keepdims=True), 1.0)
    weights_bf = (weights / totals).astype(jnp.bfloat16)
    attended = jnp.dot(weights_bf, value_rows, preferred_element_type=jnp.float32).astype(
        jnp.bfloat16
    )
    value_grad = dot_first(weights_bf, head_grad).astype(jnp.bfloat16)
    prob_grad = dot_last(head_grad, value_rows)
    row_delta = jnp.sum(
        head_grad.astype(jnp.float32) * attended.astype(jnp.float32), axis=1, keepdims=True
    )
    score_grad = (weights_bf.astype(jnp.float32) * (prob_grad - row_delta)).astype(jnp.bfloat16)
    qn_grad = jnp.dot(score_grad, k_hat, preferred_element_type=jnp.float32) * factor
    kn_grad = dot_first(score_grad, q_hat) * factor
    query_grad = norm_backward(qn_grad, q_normed, q_inv, q_scale)
    key_grad = norm_backward(kn_grad, k_normed, k_inv, k_scale)
    return (attended, query_grad, key_grad, value_grad)


def body(qkv, segment_ids, block_dest, q_gain, k_gain, out_weight, cotangent):
    peer_count = lax.axis_size("dp")
    my_index = lax.axis_index("dp")
    row_count, parts_qkv, col_width = qkv.shape
    per_device = row_count // BLK
    blocks = qkv.reshape(per_device, BLK, parts_qkv, col_width)
    seg_blocks = segment_ids.reshape(per_device, BLK)
    local_ids = jnp.arange(per_device, dtype=jnp.int32)
    peer_ids = jnp.arange(peer_count, dtype=jnp.int32)
    my_targets = (
        lax.dynamic_slice_in_dim(block_dest, my_index * per_device, per_device) // per_device
    )
    hit_table = (my_targets[None, :] == peer_ids[:, None]).astype(jnp.int32)
    chosen = jnp.sum(hit_table * local_ids[None, :], axis=1) + per_device * (
        1 - jnp.sum(hit_table, axis=1)
    )
    padded = jnp.concatenate(
        [blocks, jnp.zeros((1, BLK, parts_qkv, col_width), blocks.dtype)], axis=0
    )
    seg_padded = jnp.concatenate([seg_blocks, jnp.full((1, BLK), -1, jnp.int32)], axis=0)
    outgoing = jnp.take(padded, chosen, axis=0)
    seg_out = jnp.take(seg_padded, chosen, axis=0)
    incoming, seg_in = (
        lax.all_to_all(outgoing, "dp", split_axis=0, concat_axis=0, tiled=True),
        lax.all_to_all(seg_out, "dp", split_axis=0, concat_axis=0, tiled=True),
    )
    targets = my_index * per_device + local_ids
    all_ids = jnp.arange(block_dest.shape[0], dtype=jnp.int32)
    matches = (block_dest[None, :] == targets[:, None]).astype(jnp.int32)
    sources = jnp.sum(matches * all_ids[None, :], axis=1) // per_device
    balanced = jnp.take(incoming, sources, axis=0).reshape(row_count, parts_qkv, col_width)
    segments = jnp.take(seg_in, sources, axis=0).reshape(row_count)
    grad_rows = lax.all_gather(cotangent, "mp", axis=0, tiled=True)
    out_grad = jnp.dot(grad_rows, out_weight, preferred_element_type=jnp.float32).astype(
        jnp.bfloat16
    )
    attended_parts, query_parts, key_parts, value_parts = ([], [], [], [])
    for head_idx in range(col_width // HD):
        first_col = head_idx * HD
        columns = slice(first_col, first_col + HD)
        result = head_pass(
            balanced[:, 0, columns],
            balanced[:, 1, columns],
            balanced[:, 2, columns],
            q_gain[columns],
            k_gain[columns],
            segments,
            out_grad[:, columns],
        )
        attended_parts.append(result[0])
        query_parts.append(result[1])
        key_parts.append(result[2])
        value_parts.append(result[3])
    attended = jnp.concatenate(attended_parts, axis=1)
    qkv_grad = jnp.stack(
        [
            jnp.concatenate(query_parts, axis=1),
            jnp.concatenate(key_parts, axis=1),
            jnp.concatenate(value_parts, axis=1),
        ],
        axis=1,
    )
    partial_value = dot_last(attended, out_weight)
    summed_all = lax.psum(partial_value.astype(jnp.bfloat16), "mp").astype(jnp.float32)
    share_rows = row_count // lax.axis_size("mp")
    attn_out = lax.dynamic_slice_in_dim(
        summed_all, lax.axis_index("mp") * share_rows, share_rows, 0
    ).astype(jnp.bfloat16)
    w_grad = lax.psum_scatter(
        dot_first(grad_rows, attended).astype(jnp.bfloat16), "dp", scatter_dimension=0, tiled=True
    ).astype(jnp.float32)
    return (attn_out, qkv_grad, w_grad)


def solution(mesh):
    placed = (
        P("dp", None, "mp"),
        P("dp"),
        P(),
        P("mp"),
        P("mp"),
        P(None, "mp"),
        P(("dp", "mp"), None),
    )
    return jax.shard_map(
        body,
        mesh=mesh,
        in_specs=placed,
        out_specs=(P(("dp", "mp"), None), P("dp", None, "mp"), P("dp", "mp")),
        check_vma=False,
    )
```

profile of v0, /device:TPU:8, one launch (start us, length us, event | category | flops | bytes accessed | tf_op | source)
XLA Modules:
  0.0 613.4 jit_solution(10100269106852085507)
XLA Ops:
  7.2 0.8 and_select_fusion
  8.1 0.7 concatenate.18
  9.3 0.7 bitcast_select_fusion
  10.0 7.5 %all-to-all-start = ((s32[32,1,128]{2,1,0:T(1,128)}), s32[32,1,128]{2,1,0:T(1,128)S(1)}, u32[]{:S(2)}, u32[]{:S(2)}) async-start(s32[32,1,128]{2,1,0:T(1,128)} %bitcast.5), calls=%async_computation | async-start | bytes 32768 | tf_op jit(solution)/shard_map/all_to_all | solution.py:94
  17.5 4.3 concatenate.19
  21.9 10.0 %gather_fusion.2 = bf16[32,128,3,768]{3,1,2,0:T(8,128)(2,1)} fusion(bf16[7,128,3,768]{3,1,0,2:T(8,128)(2,1)} %concatenate.19, s32[1024]{0:T(1024)S(1)} %pad_clamp_fusion.1), kind=kCustom, calls=%fused_computation.2 | custom fusion | bytes 37748864 | tf_op jit(solution)/shard_map/jit(_take)/gather | solution.py:90
  31.9 17.2 %broadcast_select_fusion = bf16[32,128,3,768]{3,1,2,0:T(8,128)(2,1)} fusion(bf16[32,128,3,768]{3,1,2,0:T(8,128)(2,1)} %gather_fusion.2, pred[32]{0:T(512)(128)(4,1)S(1)} %compare_and_fusion.1), kind=kLoop, calls=%fused_computation.4 | loop fusion | flops 9437184 | bytes 37748768 | tf_op jit(solution)/shard_map/jit(_take)/select_n | solution.py:90
  49.1 7.6 %all-to-all-start.1 = ((bf16[32,128,3,768]{3,1,2,0:T(8,128)(2,1)}), bf16[32,128,3,768]{3,1,2,0:T(8,128)(2,1)}, u32[]{:S(2)}, u32[]{:S(2)}) async-start(bf16[32,128,3,768]{3,1,2,0:T(8,128)(2,1)} %broadcast_select_fusion), calls=%async_computation.1 | async-start | bytes 37748736 | tf_op jit(solution)/shard_map/all_to_all | solution.py:93
  56.8 0.7 all-gather.2.cloned.1.call-update
  57.9 0.6 broadcast_multiply_fusion.37
  58.5 0.6 broadcast_multiply_fusion.45
  59.7 54.5 %all-gather.2.cloned.1.call-done = bf16[768,3072]{1,0:T(8,128)(2,1)} async-done(((bf16[192,3072]{1,0:T(8,128)(2,1)}), bf16[768,3072]{1,0:T(8,128)(2,1)}) %all-gather.2.cloned.1.call-update) | async-done | bytes 4718608 | tf_op jit(solution)/shard_map/all_gather | solution.py:102
  114.2 8.7 %convolution_convert_fusion.2 = bf16[768,768]{0,1:T(8,128)(2,1)} fusion(bf16[768,3072]{1,0:T(8,128)(2,1)} %all-gather.2.cloned.1.call-done, bf16[3072,768]{1,0:T(8,128)(2,1)} %param.12), kind=kOutput, calls=%fused_computation.42 | convolution fusion | flops 3624468480 | bytes 10616832 | tf_op jit(solution)/shard_map/dot_general | solution.py:103
  122.9 236.8 %all-to-all-done.1 = bf16[32,128,3,768]{3,1,2,0:T(8,128)(2,1)} async-done(((bf16[32,128,3,768]{3,1,2,0:T(8,128)(2,1)}), bf16[32,128,3,768]{3,1,2,0:T(8,128)(2,1)}, u32[]{:S(2)}, u32[]{:S(2)}) %all-to-all-start.1) | async-done | bytes 18874400 | tf_op jit(solution)/shard_map/all_to_all | solution.py:93
  359.7 7.1 %gather_fusion.3 = bf16[6,128,3,768]{3,1,2,0:T(8,128)(2,1)S(1)} fusion(bf16[32,128,3,768]{3,1,2,0:T(8,128)(2,1)} %all-to-all-done.1, s32[1024]{0:T(1024)S(1)} %pad_clamp_fusion), kind=kCustom, calls=%fused_computation.3 | custom fusion | bytes 7077912 | tf_op jit(solution)/shard_map/jit(_take)/gather | solution.py:100
  366.9 2.0 copy.40
  368.9 6.2 %copy.41 = bf16[768,3,768]{0,2,1:T(8,128)(2,1)} copy(bf16[768,3,768]{2,0,1:T(8,128)(2,1)} %bitcast.504) | data formatting | bytes 7077888 | tf_op jit(solution)/shard_map/jit(_take)/gather | solution.py:100
  375.1 2.3 broadcast_select_fusion.1
  378.9 1.1 fusion.6
  380.0 1.7 fusion.362
  381.8 1.9 divide_convert_fusion.1
  385.8 2.1 fusion.172
  388.6 1.1 fusion.2
  389.7 1.7 fusion.358
  391.5 2.1 divide_convert_fusion.4
  397.0 2.0 fusion.142
  399.9 1.1 fusion.4
  401.0 1.7 fusion.360
  402.8 1.9 divide_convert_fusion.2
  405.4 0.7 multiply_reduce_fusion.2
  406.1 1.5 multiply_convert_fusion.2
  407.7 1.0 copy-done.67
  408.7 5.7 convolution_convert_fusion.1
  414.8 8.7 %fusion = bf16[3072,768]{0,1:T(8,128)(2,1)} fusion(bf16[768,768]{0,1:T(8,128)(2,1)} %copy-done.67, bf16[768,3072]{1,0:T(8,128)(2,1)} %all-gather.2.cloned.1.call-done), kind=kOutput, calls=%fused_computation.7 | convolution fusion | flops 3626237952 | bytes 10616832 | tf_op jit(solution)/shard_map/dot_general | solution.py:17
  423.5 1.3 convolution_multiply_fusion.7
  424.9 6.8 %copy.56 = bf16[3072,768]{1,0:T(8,128)(2,1)} copy(bf16[3072,768]{0,1:T(8,128)(2,1)} %fusion) | data formatting | bytes 9437184
  431.7 2.0 convolution_multiply_fusion.8
  433.6 3.5 fusion.188
  439.0 1.6 multiply_convert_fusion.3
  441.8 0.7 copy-done.19
  442.5 2.0 fusion.112
  445.1 0.6 broadcast_multiply_fusion.19
  446.9 0.6 broadcast_multiply_fusion.20
  450.6 0.8 broadcast_multiply_fusion.8
  451.4 0.7 broadcast_multiply_fusion.9
  452.0 0.7 broadcast_multiply_fusion.14
  452.7 0.7 broadcast_multiply_fusion.15
  453.4 0.7 broadcast_multiply_fusion.6
  454.1 0.7 broadcast_multiply_fusion.7
  454.8 0.7 broadcast_multiply_fusion.12
  455.5 0.7 broadcast_multiply_fusion.13
  456.1 0.7 broadcast_multiply_fusion.2
  456.8 0.7 broadcast_multiply_fusion.3
  457.5 0.7 broadcast_multiply_fusion
  458.2 0.7 broadcast_multiply_fusion.1
  458.9 1.1 fusion.244
  460.0 1.2 fusion.235
  461.3 1.2 fusion.226
  468.6 3.7 copy.48
  472.3 45.6 %all-reduce.4.cloned.1.call-done = bf16[768,3072]{1,0:T(8,128)(2,1)} async-done(((bf16[768,3072]{1,0:T(8,128)(2,1)}), bf16[768,3072]{1,0:T(8,128)(2,1)}) %all-reduce.4.cloned.1.call-update) | async-done | bytes 4718608 | tf_op jit(solution)/shard_map/psum | solution.py:133
  517.8 2.4 convert_convert_fusion
  520.2 84.3 %reduce-scatter.4.cloned.1.call-done = bf16[96,768]{1,0:T(8,128)(2,1)} async-done(((bf16[3072,768]{1,0:T(8,128)(2,1)}), bf16[96,768]{1,0:T(8,128)(2,1)}) %reduce-scatter.4.cloned.1.call-update) | async-done | bytes 147472
  604.5 1.1 copy.57
  605.6 0.9 copy.49
  (355 shorter events, 23.7 us)
Async XLA Ops:
  10.0 39.1 %all-to-all-start = ((s32[32,1,128]{2,1,0:T(1,128)}), s32[32,1,128]{2,1,0:T(1,128)S(1)}, u32[]{:S(2)}, u32[]{:S(2)}) async-start(s32[32,1,128]{2,1,0:T(1,128)} %bitcast.5), calls=%async_computation | async-start | bytes 32768 | tf_op jit(solution)/shard_map/all_to_all | solution.py:94
  49.1 8.4 %copy-start.116 = (s32[192]{0:T(256)S(1)}, s32[192]{0:T(256)}, u32[]{:S(2)}) copy-start(s32[192]{0:T(256)} %param.9) | copy-start | bytes 2308
  49.1 8.8 %copy-start.104 = (f32[768]{0:T(1024)S(1)}, f32[768]{0:T(1024)}, u32[]{:S(2)}) copy-start(f32[768]{0:T(1024)} %param.11) | copy-start | bytes 9220
  49.1 9.4 %copy-start.105 = (f32[768]{0:T(1024)S(1)}, f32[768]{0:T(1024)}, u32[]{:S(2)}) copy-start(f32[768]{0:T(1024)} %param.10) | copy-start | bytes 9220
  49.1 310.6 %all-to-all-start.1 = ((bf16[32,128,3,768]{3,1,2,0:T(8,128)(2,1)}), bf16[32,128,3,768]{3,1,2,0:T(8,128)(2,1)}, u32[]{:S(2)}, u32[]{:S(2)}) async-start(bf16[32,128,3,768]{3,1,2,0:T(8,128)(2,1)} %broadcast_select_fusion), calls=%async_computation.1 | async-start | bytes 37748736 | tf_op jit(solution)/shard_map/all_to_all | solution.py:93
  56.7 57.5 %all-gather.2.cloned.1.call-start = ((), (), s32[]{:S(2)}) async-start(), calls=%async_computation.4 | async-start | bytes 5898240 | tf_op jit(solution)/shard_map/all_gather | solution.py:102
  57.5 460.4 %all-reduce.4.cloned.1.call-start = ((), (), s32[]{:S(2)}) async-start(), calls=%async_computation.3 | async-start | bytes 9437184 | tf_op jit(solution)/shard_map/psum | solution.py:133
  59.7 322.0 %copy-start.44 = (pred[768]{0:T(1024)(128)(4,1)}, pred[768]{0:T(1024)(128)(4,1)S(1)}, u32[]{:S(2)}) copy-start(pred[768]{0:T(1024)(128)(4,1)S(1)} %get-tuple-element.83) | copy-start | bytes 2308
  377.9 7.9 %copy-start.57 = (f32[768]{0:T(1024)}, f32[768]{0:T(1024)S(1)}, u32[]{:S(2)}) copy-start(f32[768]{0:T(1024)S(1)} %get-tuple-element.139) | copy-start | bytes 9220
  377.9 7.8 %copy-start.59 = (f32[768]{0:T(1024)}, f32[768]{0:T(1024)S(1)}, u32[]{:S(2)}) copy-start(f32[768]{0:T(1024)S(1)} %get-tuple-element.141) | copy-start | bytes 9220
  377.9 19.0 %copy-start.37 = (f32[768]{0:T(1024)}, f32[768]{0:T(1024)S(1)}, u32[]{:S(2)}) copy-start(f32[768]{0:T(1024)S(1)} %get-tuple-element.142) | copy-start | bytes 9220
  378.2 18.8 %copy-start.46 = (f32[768]{0:T(1024)}, f32[768]{0:T(1024)S(1)}, u32[]{:S(2)}) copy-start(f32[768]{0:T(1024)S(1)} %add_rsqrt_fusion.2) | copy-start | bytes 9220
  378.2 18.8 %copy-start.48 = (f32[768]{0:T(1024)}, f32[768]{0:T(1024)S(1)}, u32[]{:S(2)}) copy-start(f32[768]{0:T(1024)S(1)} %add_rsqrt_fusion.3) | copy-start | bytes 9220
  378.2 7.5 %copy-start.69 = (f32[768]{0:T(1024)}, f32[768]{0:T(1024)S(1)}, u32[]{:S(2)}) copy-start(f32[768]{0:T(1024)S(1)} %add_rsqrt_fusion) | copy-start | bytes 9220
  378.2 7.5 %copy-start.71 = (f32[768]{0:T(1024)}, f32[768]{0:T(1024)S(1)}, u32[]{:S(2)}) copy-start(f32[768]{0:T(1024)S(1)} %add_rsqrt_fusion.1) | copy-start | bytes 9220
  385.0 12.0 %copy-start.21 = (bf16[768,768]{0,1:T(8,128)(2,1)}, bf16[768,768]{0,1:T(8,128)(2,1)S(1)}, u32[]{:S(2)}) copy-start(bf16[768,768]{0,1:T(8,128)(2,1)S(1)} %multiply_convert_fusion.1) | copy-start | bytes 3538948
  385.6 13.6 %copy-start.39 = (f32[768]{0:T(1024)}, f32[768]{0:T(1024)S(1)}, u32[]{:S(2)}) copy-start(f32[768]{0:T(1024)S(1)} %get-tuple-element.144) | copy-start | bytes 9220
  385.6 14.2 %copy-start.87 = (f32[768]{0:T(1024)}, f32[768]{0:T(1024)S(1)}, u32[]{:S(2)}) copy-start(f32[768]{0:T(1024)S(1)} %get-tuple-element.143) | copy-start | bytes 9220
  385.6 13.5 %copy-start.64 = (f32[768]{0:T(1024)}, f32[768]{0:T(1024)S(1)}, u32[]{:S(2)}) copy-start(f32[768]{0:T(1024)S(1)} %get-tuple-element.146) | copy-start | bytes 9220
  385.7 14.2 %copy-start.90 = (f32[768]{0:T(1024)}, f32[768]{0:T(1024)S(1)}, u32[]{:S(2)}) copy-start(f32[768]{0:T(1024)S(1)} %get-tuple-element.145) | copy-start | bytes 9220
  385.7 10.8 %copy-start.61 = (f32[768]{0:T(1024)}, f32[768]{0:T(1024)S(1)}, u32[]{:S(2)}) copy-start(f32[768]{0:T(1024)S(1)} %get-tuple-element.147) | copy-start | bytes 9220
  385.7 11.3 %copy-start.93 = (f32[768]{0:T(1024)}, f32[768]{0:T(1024)S(1)}, u32[]{:S(2)}) copy-start(f32[768]{0:T(1024)S(1)} %get-tuple-element.148) | copy-start | bytes 9220
  385.7 11.3 %copy-start.42 = (f32[768]{0:T(1024)}, f32[768]{0:T(1024)S(1)}, u32[]{:S(2)}) copy-start(f32[768]{0:T(1024)S(1)} %get-tuple-element.149) | copy-start | bytes 9220
  385.7 11.3 %copy-start.66 = (f32[768]{0:T(1024)}, f32[768]{0:T(1024)S(1)}, u32[]{:S(2)}) copy-start(f32[768]{0:T(1024)S(1)} %get-tuple-element.150) | copy-start | bytes 9220
  387.9 9.1 %copy-start.54 = (f32[768]{0:T(1024)}, f32[768]{0:T(1024)S(1)}, u32[]{:S(2)}) copy-start(f32[768]{0:T(1024)S(1)} %add_rsqrt_fusion.11) | copy-start | bytes 9220
  387.9 8.6 %copy-start.51 = (f32[768]{0:T(1024)}, f32[768]{0:T(1024)S(1)}, u32[]{:S(2)}) copy-start(f32[768]{0:T(1024)S(1)} %add_rsqrt_fusion.8) | copy-start | bytes 9220
  388.0 9.1 %copy-start.73 = (f32[768]{0:T(1024)}, f32[768]{0:T(1024)S(1)}, u32[]{:S(2)}) copy-start(f32[768]{0:T(1024)S(1)} %add_rsqrt_fusion.9) | copy-start | bytes 9220
  402.8 6.0 slice-start
  404.7 4.0 slice-start.1
  414.4 9.1 %copy-start.38 = (f32[768]{0:T(1024)S(1)}, f32[768]{0:T(1024)}, u32[]{:S(2)}) copy-start(f32[768]{0:T(1024)} %copy-done.37) | copy-start | bytes 9220
  414.4 190.1 %reduce-scatter.4.cloned.1.call-start = ((), (), s32[]{:S(2)}) async-start(), calls=%async_computation.5 | async-start | bytes 4866048
  414.7 8.8 %copy-start.22 = (bf16[768,768]{0,1:T(8,128)(2,1)S(1)}, bf16[768,768]{0,1:T(8,128)(2,1)}, u32[]{:S(2)}) copy-start(bf16[768,768]{0,1:T(8,128)(2,1)} %copy-done.21) | copy-start | bytes 3538948
  414.7 8.8 %copy-start.49 = (f32[768]{0:T(1024)S(1)}, f32[768]{0:T(1024)}, u32[]{:S(2)}) copy-start(f32[768]{0:T(1024)} %copy-done.48) | copy-start | bytes 9220
  414.8 8.8 %copy-start.110 = (f32[128]{0:T(128)S(1)}, f32[128]{0:T(128)}, u32[]{:S(2)}) copy-start(f32[128]{0:T(128)} %get-tuple-element.122) | copy-start | bytes 1540
  414.8 8.8 %copy-start.125 = (f32[128]{0:T(128)S(1)}, f32[128]{0:T(128)}, u32[]{:S(2)}) copy-start(f32[128]{0:T(128)} %get-tuple-element.99) | copy-start | bytes 1540
  431.6 6.8 %copy-start.12 = (bf16[768,768]{0,1:T(8,128)(2,1)S(1)}, bf16[768,768]{0,1:T(8,128)(2,1)}, u32[]{:S(2)}) copy-start(bf16[768,768]{0,1:T(8,128)(2,1)} %copy-done.11) | copy-start | bytes 3538948
  431.6 6.8 %copy-start.74 = (f32[768]{0:T(1024)S(1)}, f32[768]{0:T(1024)}, u32[]{:S(2)}) copy-start(f32[768]{0:T(1024)} %copy-done.73) | copy-start | bytes 9220
  431.6 6.8 %copy-start.94 = (f32[768]{0:T(1024)S(1)}, f32[768]{0:T(1024)}, u32[]{:S(2)}) copy-start(f32[768]{0:T(1024)} %copy-done.93) | copy-start | bytes 9220
  431.6 6.8 %copy-start.121 = (f32[128]{0:T(128)S(1)}, f32[128]{0:T(128)}, u32[]{:S(2)}) copy-start(f32[128]{0:T(128)} %get-tuple-element.101) | copy-start | bytes 1540
  431.6 6.8 %copy-start.123 = (f32[128]{0:T(128)S(1)}, f32[128]{0:T(128)}, u32[]{:S(2)}) copy-start(f32[128]{0:T(128)} %get-tuple-element.119) | copy-start | bytes 1540
  433.6 5.3 copy-start.32
  433.6 5.4 copy-start.9
  433.6 5.4 copy-start.68
  437.2 3.5 copy-start.120
  441.7 4.0 copy-start.103
  441.7 4.6 copy-start.102
  441.7 5.2 copy-start.101
  441.7 5.7 copy-start.100
  441.7 7.5 %copy-start.99 = (f32[768]{0:T(1024)S(1)}, f32[768]{0:T(1024)}, u32[]{:S(2)}) copy-start(f32[768]{0:T(1024)} %get-tuple-element.25) | copy-start | bytes 9220
  441.7 8.1 %copy-start.98 = (f32[768]{0:T(1024)S(1)}, f32[768]{0:T(1024)}, u32[]{:S(2)}) copy-start(f32[768]{0:T(1024)} %get-tuple-element.63) | copy-start | bytes 9220
  450.5 12.0 %copy-start.30 = (f32[768,128]{0,1:T(8,128)S(1)}, f32[768,128]{0,1:T(8,128)}, u32[]{:S(2)}) copy-start(f32[768,128]{0,1:T(8,128)} %copy-done.29) | copy-start | bytes 1179652
  450.5 12.0 %copy-start.36 = (f32[768,128]{0,1:T(8,128)S(1)}, f32[768,128]{0,1:T(8,128)}, u32[]{:S(2)}) copy-start(f32[768,128]{0,1:T(8,128)} %get-tuple-element.137) | copy-start | bytes 1179652
  450.5 12.0 %copy-start.43 = (f32[768]{0:T(1024)S(1)}, f32[768]{0:T(1024)}, u32[]{:S(2)}) copy-start(f32[768]{0:T(1024)} %copy-done.42) | copy-start | bytes 9220
  450.5 12.0 %copy-start.80 = (f32[768]{0:T(1024)S(1)}, f32[768]{0:T(1024)}, u32[]{:S(2)}) copy-start(f32[768]{0:T(1024)} %copy-done.78) | copy-start | bytes 9220
  450.5 12.0 %copy-start.83 = (f32[768]{0:T(1024)S(1)}, f32[768]{0:T(1024)}, u32[]{:S(2)}) copy-start(f32[768]{0:T(1024)} %broadcast_multiply_fusion.16) | copy-start | bytes 9220
  450.5 12.0 %copy-start.84 = (f32[768]{0:T(1024)S(1)}, f32[768]{0:T(1024)}, u32[]{:S(2)}) copy-start(f32[768]{0:T(1024)} %broadcast_multiply_fusion.17) | copy-start | bytes 9220
  450.5 12.0 %copy-start.85 = (f32[768]{0:T(1024)S(1)}, f32[768]{0:T(1024)}, u32[]{:S(2)}) copy-start(f32[768]{0:T(1024)} %broadcast_multiply_fusion.10) | copy-start | bytes 9220
  450.5 12.0 %copy-start.86 = (f32[768]{0:T(1024)S(1)}, f32[768]{0:T(1024)}, u32[]{:S(2)}) copy-start(f32[768]{0:T(1024)} %broadcast_multiply_fusion.11) | copy-start | bytes 9220
  450.5 12.0 %copy-start.92 = (f32[768]{0:T(1024)S(1)}, f32[768]{0:T(1024)}, u32[]{:S(2)}) copy-start(f32[768]{0:T(1024)} %copy-done.90) | copy-start | bytes 9220
  450.5 12.2 %copy-start.31 = (f32[768,128]{0,1:T(8,128)S(1)}, f32[768,128]{0,1:T(8,128)}, u32[]{:S(2)}) copy-start(f32[768,128]{0,1:T(8,128)} %get-tuple-element.131) | copy-start | bytes 1179652
  450.6 12.2 %copy-start.35 = (f32[768,128]{0,1:T(8,128)S(1)}, f32[768,128]{0,1:T(8,128)}, u32[]{:S(2)}) copy-start(f32[768,128]{0,1:T(8,128)} %copy-done.34) | copy-start | bytes 1179652
  450.6 12.2 %copy-start.50 = (f32[768]{0:T(1024)S(1)}, f32[768]{0:T(1024)}, u32[]{:S(2)}) copy-start(f32[768]{0:T(1024)} %copy-done.48) | copy-start | bytes 9220
  450.6 12.2 %copy-start.53 = (f32[768]{0:T(1024)S(1)}, f32[768]{0:T(1024)}, u32[]{:S(2)}) copy-start(f32[768]{0:T(1024)} %copy-done.51) | copy-start | bytes 9220
  450.6 12.2 %copy-start.63 = (f32[768]{0:T(1024)S(1)}, f32[768]{0:T(1024)}, u32[]{:S(2)}) copy-start(f32[768]{0:T(1024)} %copy-done.61) | copy-start | bytes 9220
  (74 other events, 135.5 us)
Sparse Core Ops, SparseCore 0:
  59.2 54.9 all-gather.1
  414.5 103.2 all-reduce.3
  521.6 82.8 reduce-scatter.3
where the time goes:
time: 621 us; the launch traced here: 613 us
  waiting for transfers between devices  422 us (68%)
  other arithmetic  57.8 us (9%)
  matrix products  54.2 us (9%)
  local copies, waits for them, and re-layouts  47.6 us (8%)
  between operations  16.4 us (3%)
  starting transfers between devices  15.5 us (2%)
    all_to_all x1, waiting for transfers between devices, body(): lax.all_to_all(outgoing, 'dp', split_axis=0, concat_axis=0, tiled=True)  237 us
    unnamed x4, waiting for transfers between devices  85 us
    all_gather x1, waiting for transfers between devices, body(): grad_rows = lax.all_gather(cotangent, 'mp', axis=0, tiled=True)  54.5 us
    psum x1, waiting for transfers between devices, body(): lax.psum(partial_value.astype(jnp.bfloat16), 'mp').astype(jnp.float32)  45.6 us
    dot_general x13, matrix products, dot_first(): lax.dot_general(left, right, (((0,), (0,)), ((), ())), preferred_element_...  20.4 us
    select_n x1, other arithmetic, body(): outgoing = jnp.take(padded, chosen, axis=0)  17.2 us
    unnamed x271, local copies, waits for them, and re-layouts  15.9 us
    dot_general x13, matrix products, dot_last(): lax.dot_general(left, right, (((1,), (1,)), ((), ())), preferred_element_...  15.9 us
  transfers between devices with their start and end apart: 5, of which 4 were waited for; matrix products, arithmetic and copies ran while one was open for 16% of the time, Pallas kernels for 0%

commit v1 on v0

v1 whole, which is shorter than its diff:
```python
import functools
import math

import jax
import jax.numpy as jnp
from jax import lax
from jax.experimental import pallas as pl
from jax.experimental.pallas import tpu as pltpu
from jax.sharding import Mesh
from jax.sharding import PartitionSpec as P

HD = 128
BLK = 128


NORM_EPS = 1e-06
MASKED_SCORE = -1e30
LOG2_E = math.log2(math.e)
DP = ("x", "y", "core")
FORWARD_ROWS = 384
FORWARD_HEADS = 3
BACKWARD_ROWS = 768
VMEM_LIMIT = 56 * 1024 * 1024
LITTLE = pl.CostEstimate(flops=1, bytes_accessed=1, transcendentals=0)
LARGE = pl.CostEstimate(flops=10**12, bytes_accessed=10**9, transcendentals=0)


def dot_first(left, right):
    return lax.dot_general(
        left, right, (((0,), (0,)), ((), ())), preferred_element_type=jnp.float32
    )


def dot_last(left, right):
    return lax.dot_general(
        left, right, (((1,), (1,)), ((), ())), preferred_element_type=jnp.float32
    )


def layer_norm(values, norm_gain):
    centred = values - jnp.mean(values, axis=1, keepdims=True)
    inv_scale = lax.rsqrt(jnp.mean(centred * centred, axis=1, keepdims=True) + NORM_EPS)
    normed = centred * inv_scale
    return (normed, inv_scale, (normed * norm_gain).astype(jnp.bfloat16))


def norm_backward(upstream, normed, inv_scale, norm_gain):
    scaled = upstream * norm_gain
    centred = scaled - jnp.mean(scaled, axis=1, keepdims=True)
    projection_term = normed * jnp.mean(scaled * normed, axis=1, keepdims=True)
    return (inv_scale * (centred - projection_term)).astype(jnp.bfloat16)


def in_row_order(ref, columns):
    cuts, span, _ = ref.shape[0], ref.shape[3], ref.shape[4]
    rows8 = BLK // cuts
    tiles = ref[:, 0, 0, :, columns].astype(jnp.float32).reshape(cuts, span // rows8, rows8, HD)
    return jnp.concatenate(
        [tiles[:, pos].reshape(BLK, HD) for pos in range(span // rows8)], axis=0
    )


def forward_kernel(
    groups, here_ref, q_ref, k_ref, v_ref, seg_col, seg_row, qg_ref, kg_ref, weight_ref,
    att_ref, prob_ref, *refs,
):
    at_step = pl.program_id(0)
    rows, width = att_ref.shape[0], q_ref.shape[-1]

    def attend(group):
        factor = LOG2_E / math.sqrt(HD)
        keys_image = seg_row[...]
        keys_image = jnp.where(keys_image >= 0, keys_image, -2)
        heads = [slice(first, first + HD) for first in range(0, width, HD)]
        q_hats = [layer_norm(in_row_order(q_ref, at), qg_ref[:, at])[2] for at in heads]
        k_hats = [layer_norm(in_row_order(k_ref, at), kg_ref[:, at])[2] for at in heads]
        values = [in_row_order(v_ref, at).astype(jnp.bfloat16) for at in heads]
        tasks = [
            (head, slice(start, start + FORWARD_ROWS))
            for head in range(len(heads))
            for start in range(0, rows, FORWARD_ROWS)
        ]

        def scores_of(head, block):
            return dot_last(q_hats[head][block], k_hats[head])

        ready = scores_of(*tasks[0])
        for at, (head, block) in enumerate(tasks):
            scores = ready
            if at + 1 < len(tasks):
                ready = scores_of(*tasks[at + 1])
            image = seg_col[block]
            masked = jnp.where(image == keys_image, scores, MASKED_SCORE)
            top = jnp.max(masked, axis=1, keepdims=True)
            weights = jnp.exp2((masked - top) * factor)
            totals = jnp.maximum(jnp.sum(weights, axis=1, keepdims=True), 1.0)
            scale = jnp.where(image >= 0, 1.0 / totals, 0.0)
            probs = (weights * scale).astype(jnp.bfloat16)
            prob_ref[head, block] = probs
            first = group * width + head * HD
            att_ref[block, first : first + HD] = jnp.dot(
                probs, values[head], preferred_element_type=jnp.float32
            ).astype(jnp.bfloat16)

    for group in range(groups):
        pl.when(at_step == group)(functools.partial(attend, group))

    part_refs, back_ref, turned = refs[:-2], refs[-2], refs[-1]
    places = len(part_refs)
    share = rows // places

    @pl.when(at_step == groups)
    def _():
        for by in range(places):
            first = pl.multiple_of((here_ref[0] + by) % places * share, share)
            block = att_ref[pl.ds(first, share)]
            turned[by * share : (by + 1) * share] = block
            back = (places - by) % places
            back_ref[back * share : (back + 1) * share] = block

    @pl.when(at_step >= groups)
    def _():
        sums = dot_last(turned[...], weight_ref[...]).astype(jnp.bfloat16)
        for by, part_ref in enumerate(part_refs):
            part_ref[...] = sums[by * share : (by + 1) * share]


def backward_kernel(step, q_ref, k_ref, v_ref, prob_ref, grad_ref, att_ref, qg_ref, kg_ref, out_ref):
    factor = 1.0 / math.sqrt(HD)
    q_normed, q_inv, q_hat = layer_norm(in_row_order(q_ref, slice(0, HD)), qg_ref[...])
    k_normed, k_inv, k_hat = layer_norm(in_row_order(k_ref, slice(0, HD)), kg_ref[...])
    values = in_row_order(v_ref, slice(0, HD)).astype(jnp.bfloat16)
    rows = att_ref.shape[0]
    key_sum = jnp.zeros((HD, rows), jnp.float32)
    value_sum = jnp.zeros((HD, rows), jnp.float32)
    for start in range(0, rows, step):
        block = slice(start, start + step)
        grads = grad_ref[block]
        wide = grads.astype(jnp.float32)
        probs = prob_ref[0, block]
        delta = jnp.sum(wide * att_ref[block].astype(jnp.float32), axis=1, keepdims=True)
        prob_grad = dot_last(grads, values)
        score_grad = (probs.astype(jnp.float32) * (prob_grad - delta)).astype(jnp.bfloat16)
        qn_grad = jnp.dot(score_grad, k_hat, preferred_element_type=jnp.float32) * factor
        out_ref[0, block] = norm_backward(qn_grad, q_normed[block], q_inv[block], qg_ref[...])
        value_sum += jnp.dot(
            wide.T.astype(jnp.bfloat16), probs, preferred_element_type=jnp.float32
        )
        key_sum += jnp.dot(
            q_hat[block].astype(jnp.float32).T.astype(jnp.bfloat16),
            score_grad,
            preferred_element_type=jnp.float32,
        )
    out_ref[2] = value_sum.T.astype(jnp.bfloat16)
    out_ref[1] = norm_backward(key_sum.T * factor, k_normed, k_inv, kg_ref[...])


def part_specs(cuts, span, groups, width):
    per_half = groups // 2

    def spec(part):
        def place(step, *_):
            group = jnp.minimum(step, groups - 1)
            return (0, group // per_half, part, 0, group % per_half)

        return pl.BlockSpec((cuts, 1, 1, span, width), place)

    return [spec(part) for part in range(3)]


def attention_forward(landed, segments, q_gain, k_gain, out_weight, here, places):
    cuts, _, _, span, half = landed.shape
    rows, heads = cuts * span, 2 * half // HD
    groups, width = heads // FORWARD_HEADS, FORWARD_HEADS * HD
    d_out = out_weight.shape[0]
    blocks = 4
    share = rows // places
    gain_spec = pl.BlockSpec((1, width), lambda step, here: (0, jnp.minimum(step, groups - 1)))

    def column(step):
        return jnp.maximum(step - groups, 0)

    return pl.pallas_call(
        functools.partial(forward_kernel, groups),
        grid_spec=pltpu.PrefetchScalarGridSpec(
        num_scalar_prefetch=1,
        grid=(groups + blocks,),
        in_specs=part_specs(cuts, span, groups, width)
        + [
            pl.BlockSpec((rows, 1), lambda step, here: (0, 0)),
            pl.BlockSpec((1, rows), lambda step, here: (0, 0)),
            gain_spec,
            gain_spec,
            pl.BlockSpec((d_out // blocks, heads * HD), lambda step, here: (column(step), 0)),
        ],
        out_specs=[
            pl.BlockSpec((rows, heads * HD), lambda step, here: (0, 0)),
            pl.BlockSpec(
                (FORWARD_HEADS, rows, rows), lambda step, here: (jnp.minimum(step, groups - 1), 0, 0)
            ),
        ]
        + [pl.BlockSpec((share, d_out // blocks), lambda step, here: (0, column(step)))] * places
        + [pl.BlockSpec((rows, heads * HD), lambda step, here: (0, 0))],
        scratch_shapes=[pltpu.VMEM((rows, heads * HD), jnp.bfloat16)],
        ),
        out_shape=[
            jax.ShapeDtypeStruct((rows, heads * HD), jnp.bfloat16),
            jax.ShapeDtypeStruct((heads, rows, rows), jnp.bfloat16),
        ]
        + [jax.ShapeDtypeStruct((share, d_out), jnp.bfloat16)] * places
        + [jax.ShapeDtypeStruct((rows, heads * HD), jnp.bfloat16)],
        compiler_params=pltpu.CompilerParams(vmem_limit_bytes=VMEM_LIMIT),
        cost_estimate=pl.CostEstimate(
            flops=4 * heads * rows * rows * HD + 2 * rows * d_out * heads * HD,
            bytes_accessed=2 * heads * rows * (rows + 4 * HD) + 4 * rows * d_out,
            transcendentals=heads * rows * rows,
        ),
        name="attention_forward",
    )(
        here.reshape(1).astype(jnp.int32),
        landed,
        landed,
        landed,
        segments[:, None],
        segments[None, :],
        q_gain[None, :],
        k_gain[None, :],
        out_weight,
    )


def attention_backward(landed, probs, out_grad, attended, q_gain, k_gain):
    cuts, _, _, span, half = landed.shape
    rows, heads = cuts * span, 2 * half // HD
    gain_spec = pl.BlockSpec((1, HD), lambda head: (0, head))
    row_spec = pl.BlockSpec((rows, HD), lambda head: (0, head))
    return pl.pallas_call(
        functools.partial(backward_kernel, BACKWARD_ROWS),
        grid=(heads,),
        in_specs=part_specs(cuts, span, heads, HD)
        + [
            pl.BlockSpec((1, rows, rows), lambda head: (head, 0, 0)),
            row_spec,
            row_spec,
            gain_spec,
            gain_spec,
        ],
        out_specs=pl.BlockSpec((3, rows, HD), lambda head: (0, 0, head)),
        out_shape=jax.ShapeDtypeStruct((3, rows, heads * HD), jnp.bfloat16),
        compiler_params=pltpu.CompilerParams(vmem_limit_bytes=VMEM_LIMIT),
        cost_estimate=LARGE,
        name="attention_backward",
    )(landed, landed, landed, probs, out_grad, attended, q_gain[None, :], k_gain[None, :])


def cut_kernel(rows_ref, out_ref):
    cuts, span = out_ref.shape[0], out_ref.shape[3]
    rows8 = BLK // cuts
    tiles = rows_ref[0].astype(jnp.float32).reshape(span // rows8, cuts, rows8, -1)
    for cut in range(cuts):
        out_ref[cut, 0, 0] = tiles[:, cut].reshape(span, -1).astype(jnp.bfloat16)


def cut_blocks(planes, cuts):
    parts, rows, width = planes.shape
    span, half = rows // cuts, width // 2
    return pl.pallas_call(
        cut_kernel,
        grid=(parts, 2),
        in_specs=[pl.BlockSpec((1, rows, half), lambda part, side: (part, 0, side))],
        out_specs=pl.BlockSpec(
            (cuts, 1, 1, span, half), lambda part, side: (0, side, part, 0, 0)
        ),
        out_shape=jax.ShapeDtypeStruct((cuts, 2, parts, span, half), jnp.bfloat16),
        compiler_params=pltpu.CompilerParams(vmem_limit_bytes=VMEM_LIMIT),
        cost_estimate=pl.CostEstimate(
            flops=0, bytes_accessed=4 * parts * rows * width, transcendentals=0
        ),
        name="cut_blocks",
    )(planes)


def grad_kernel(here_ref, *refs):
    pieces, (weight_ref, grad_ref, columns_ref, total) = refs[:-4], refs[-4:]
    places, step = len(pieces), pl.program_id(0)
    rows = jnp.concatenate([piece[...].astype(jnp.float32) for piece in pieces], axis=0)
    columns_ref[...] = rows.T.astype(jnp.bfloat16)
    product = jnp.dot(
        rows.astype(jnp.bfloat16), weight_ref[...], preferred_element_type=jnp.float32
    )

    @pl.when(step == 0)
    def _():
        total[...] = product

    @pl.when(step > 0)
    def _():
        total[...] += product

    @pl.when(step == pl.num_programs(0) - 1)
    def _():
        share = pieces[0].shape[0]
        for back in range(places):
            first = pl.multiple_of((here_ref[0] + places - back) % places * share, share)
            grad_ref[pl.ds(first, share)] = total[back * share : (back + 1) * share].astype(
                jnp.bfloat16
            )


def grad_products(here, pieces, out_weight):
    places = len(pieces)
    share, d_out = pieces[0].shape
    width = out_weight.shape[1]
    rows, step = places * share, 768
    return pl.pallas_call(
        grad_kernel,
        grid_spec=pltpu.PrefetchScalarGridSpec(
            num_scalar_prefetch=1,
            grid=(d_out // step,),
            in_specs=[pl.BlockSpec((share, step), lambda at, here: (0, at))] * places
            + [pl.BlockSpec((step, width), lambda at, here: (at, 0))],
            out_specs=[
                pl.BlockSpec((rows, width), lambda at, here: (0, 0)),
                pl.BlockSpec((step, rows), lambda at, here: (at, 0)),
            ],
            scratch_shapes=[pltpu.VMEM((rows, width), jnp.float32)],
        ),
        out_shape=[
            jax.ShapeDtypeStruct((rows, width), jnp.bfloat16),
            jax.ShapeDtypeStruct((d_out, rows), jnp.bfloat16),
        ],
        compiler_params=pltpu.CompilerParams(vmem_limit_bytes=VMEM_LIMIT),
        cost_estimate=LITTLE,
        name="grad_products",
    )(here.reshape(1).astype(jnp.int32), *pieces, out_weight)


def weight_kernel(core_ref, cot_ref, att_ref, out_ref):
    peers, _, share, rows = cot_ref.shape
    terms = jnp.dot(
        cot_ref[...].reshape(peers * share, rows),
        att_ref[...],
        preferred_element_type=jnp.float32,
    )
    out_ref[...] = terms.astype(jnp.bfloat16).reshape(out_ref.shape)


def weight_terms(parity, grad_columns, attended, peers):
    d_out, rows = grad_columns.shape
    width = attended.shape[1]
    share = d_out // peers
    step = peers // 4
    block = pl.BlockSpec((step, share, width), lambda at, core: (at, 0, 0))
    return pl.pallas_call(
        weight_kernel,
        grid_spec=pltpu.PrefetchScalarGridSpec(
            num_scalar_prefetch=1,
            grid=(2,),
            in_specs=[
                pl.BlockSpec((step, 1, share, rows), lambda at, core: (at, core[0], 0, 0)),
                pl.BlockSpec((rows, width), lambda at, core: (0, 0)),
            ],
            out_specs=block,
        ),
        out_shape=jax.ShapeDtypeStruct((peers // 2, share, width), jnp.bfloat16),
        compiler_params=pltpu.CompilerParams(vmem_limit_bytes=VMEM_LIMIT),
        cost_estimate=LARGE,
        name="weight_terms",
    )(
        parity.reshape(1).astype(jnp.int32),
        grad_columns.reshape(peers // 2, 2, share, rows),
        attended,
    )


def turn(size, by):
    return [(at, (at + by) % size) for at in range(size)]


def gathered(own, axis):
    size = lax.axis_size(axis)
    return jnp.stack([own] + [lax.ppermute(own, axis, turn(size, by)) for by in range(1, size)])


def body(qkv, segment_ids, block_dest, q_gain, k_gain, out_weight, cotangent):
    peers = lax.axis_size(DP)
    my_index = lax.axis_index(DP)
    row_count, parts_qkv, col_width = qkv.shape
    per_device = row_count // BLK
    n_blocks = block_dest.shape[0]
    cuts = peers // 2
    rows8 = BLK // cuts
    half = col_width // 2

    all_ids = jnp.arange(n_blocks, dtype=jnp.int32)
    source_of = jnp.sum(
        (block_dest[None, :] == all_ids[:, None]).astype(jnp.int32) * all_ids[None, :], axis=1
    )
    size_x, size_y, size_core = (lax.axis_size(axis) for axis in DP)
    here_x, here_y, here_core = (lax.axis_index(axis) for axis in DP)
    seg_plane = gathered(gathered(segment_ids.reshape(per_device, BLK), "core"), "y")
    seg_plane = seg_plane.reshape(size_y * size_core * per_device, BLK)

    sources = source_of.reshape(peers, 1, per_device)
    part_ids = jnp.arange(parts_qkv, dtype=jnp.int32)[None, :, None]
    piece_of = (
        (sources // per_device) * (parts_qkv * per_device)
        + part_ids * per_device
        + sources % per_device
    ).reshape(-1)

    places = lax.axis_size("mp")
    here = lax.axis_index("mp")
    pieces_cot = [cotangent] + [
        lax.ppermute(cotangent, "mp", turn(places, by)) for by in range(1, places)
    ]

    planes = jnp.transpose(qkv, (1, 0, 2))
    pieces = cut_blocks(planes, cuts).reshape(peers, parts_qkv, per_device * rows8, half)
    spread = lax.all_to_all(pieces, DP, split_axis=0, concat_axis=0, tiled=True)
    ordered = jnp.take(
        spread.reshape(n_blocks * parts_qkv, rows8, half), piece_of, axis=0, mode="clip"
    ).reshape(pieces.shape)
    near = (pieces_cot[1], pieces_cot[places - 1])
    ordered, seg_plane, near = lax.optimization_barrier((ordered, seg_plane, near))
    pieces_cot[1], pieces_cot[places - 1] = near
    landed = lax.all_to_all(ordered, DP, split_axis=0, concat_axis=0, tiled=True)
    def images_for(plane, by):
        there = ((here_x + by) % size_x * size_y + here_y) * size_core + here_core
        wanted = lax.dynamic_slice_in_dim(source_of, there * per_device, per_device)
        holder = wanted // per_device
        back_y = (here_y - holder // size_core) % size_y
        back_core = (here_core - holder) % size_core
        row = (back_y * size_core + back_core) * per_device + wanted % per_device
        row = jnp.where(holder // (size_y * size_core) == here_x, row, -1)
        plane_ids = jnp.arange(plane.shape[0], dtype=jnp.int32)
        return jnp.sum(
            jnp.where(row[:, None, None] == plane_ids[None, :, None], plane[None], 0), axis=1
        )

    images = [images_for(seg_plane, by) for by in range(size_x)]
    out_grad, grad_columns = grad_products(here, pieces_cot, out_weight)
    images, near = lax.optimization_barrier((images, near))
    images = [images[0]] + [
        lax.ppermute(images[by], "x", turn(size_x, by)) for by in range(1, size_x)
    ]
    landed, out_grad, grad_columns = lax.optimization_barrier((landed, out_grad, grad_columns))
    segments = sum(images).reshape(row_count)
    landed = landed.reshape(cuts, 2, parts_qkv, per_device * rows8, half)

    attended, probs, *partials, attended_back = attention_forward(
        landed, segments, q_gain, k_gain, out_weight, here, places
    )
    partials = [partials[0]] + [
        lax.ppermute(partials[by], "mp", turn(places, by)) for by in range(1, places)
    ]

    core = lax.axis_index("core")
    given = weight_terms(1 - core, grad_columns, attended_back, peers)
    taken = lax.ppermute(given, "core", turn(2, 1))
    kept = weight_terms(core, grad_columns, attended_back, peers)
    pair = (kept.astype(jnp.float32) + taken.astype(jnp.float32)).astype(jnp.bfloat16)
    probs, pair = lax.optimization_barrier((probs, pair))
    terms = lax.all_to_all(pair, ("x", "y"), split_axis=0, concat_axis=0, tiled=True)
    planes_grad = attention_backward(landed, probs, out_grad, attended, q_gain, k_gain)
    partials, planes_grad = lax.optimization_barrier((partials, planes_grad))
    attn_out = sum(part.astype(jnp.float32) for part in partials).astype(jnp.bfloat16)
    w_grad = jnp.sum(terms.astype(jnp.float32), axis=0)
    qkv_grad = jnp.transpose(planes_grad, (1, 0, 2))
    return (attn_out, qkv_grad, w_grad)


def solution(mesh):
    grid = Mesh(mesh.devices.reshape(4, 4, 2, 4), ("x", "y", "core", "mp"))
    rows = ("x", "y", "core", "mp")
    placed = (
        P(DP, None, "mp"),
        P(DP),
        P(),
        P("mp"),
        P("mp"),
        P(None, "mp"),
        P(rows, None),
    )
    return jax.shard_map(
        body,
        mesh=grid,
        in_specs=placed,
        out_specs=(P(rows, None), P(DP, None, "mp"), P(DP, "mp")),
        check_vma=False,
    )
```

time: 621 us -> 200 us (0.32); the launches traced: 613 us -> 199 us
  waiting for transfers between devices: 422 us -> 65.6 us
  Pallas kernels: 0 us -> 58.5 us
  matrix products: 54.2 us -> 0 us
  other arithmetic: 57.8 us -> 16.3 us
  local copies, waits for them, and re-layouts: 47.6 us -> 14.1 us
  starting transfers between devices: 15.5 us -> 44 us
  between operations: 16.4 us -> 0.75 us
    all_to_all x2 -> x3, waiting for transfers between devices: 237 us -> 3.06 us  [the longest x1 3.06 us: body(): spread = lax.all_to_all(pieces, DP, split_axis=0, concat_axis=0, tiled=True)]
    unnamed x4 -> x0, waiting for transfers between devices: 85 us -> none
    ppermute x0 -> x14, waiting for transfers between devices: none -> 62.6 us  [the longest x4 25 us: gathered(): lax.ppermute(own, axis, turn(size, by))]
    pallas_call x0 -> x6, Pallas kernels: none -> 58.5 us  [the longest x1 19.6 us: attention_forward(): pl.pallas_call(functools.partial(forward_kernel, groups), grid_spec=pltpu...]
    all_gather x1 -> x0, waiting for transfers between devices: 54.5 us -> none  [body(): grad_rows = lax.all_gather(cotangent, 'mp', axis=0, tiled=True)]
    dot_general x39 -> x0, matrix products: 54.2 us -> none  [the longest x13 20.4 us: dot_first(): lax.dot_general(left, right, (((0,), (0,)), ((), ())), preferred_element_...]
    psum x1 -> x0, waiting for transfers between devices: 45.6 us -> none  [body(): lax.psum(partial_value.astype(jnp.bfloat16), 'mp').astype(jnp.float32)]
    ppermute x0 -> x14, starting transfers between devices: none -> 24.6 us  [the longest x3 8.06 us: body(): lax.ppermute(cotangent, 'mp', turn(places, by))]
  transfers between devices with their start and end apart: 5 -> 17, of which waited for: 4 -> 7; matrix products, arithmetic and copies ran while one was open for 16% -> 13% of each run, Pallas kernels for 0% -> 17%
where the time goes in v1:
time: 200 us; the launch traced here: 199 us
  waiting for transfers between devices  65.6 us (33%)
  Pallas kernels  58.5 us (29%)
  starting transfers between devices  44 us (22%)
  other arithmetic  16.3 us (8%)
  local copies, waits for them, and re-layouts  14.1 us (7%)
    ppermute x4, waiting for transfers between devices, gathered(): lax.ppermute(own, axis, turn(size, by))  25 us
    pallas_call x1, Pallas kernels, attention_forward(): pl.pallas_call(functools.partial(forward_kernel, groups), grid_spec=pltpu...  19.6 us
    ppermute x3, waiting for transfers between devices, body(): lax.ppermute(cotangent, 'mp', turn(places, by))  16.6 us
    ppermute x3, waiting for transfers between devices, body(): lax.ppermute(partials[by], 'mp', turn(places, by))  15.7 us
    pallas_call x1, Pallas kernels, attention_backward(): pl.pallas_call(functools.partial(backward_kernel, BACKWARD_ROWS), grid=(h...  14.4 us
    pallas_call x2, Pallas kernels, weight_terms(): pl.pallas_call(weight_kernel, grid_spec=pltpu.PrefetchScalarGridSpec(num_...  9.71 us
    pallas_call x1, Pallas kernels, grad_products(): pl.pallas_call(grad_kernel, grid_spec=pltpu.PrefetchScalarGridSpec(num_sc...  9.29 us
    ppermute x3, starting transfers between devices, body(): lax.ppermute(cotangent, 'mp', turn(places, by))  8.06 us
  transfers between devices with their start and end apart: 17, of which 7 were waited for; matrix products, arithmetic and copies ran while one was open for 13% of the time, Pallas kernels for 17%

profile of v1, /device:TPU:8, one launch (start us, length us, event | category | flops | bytes accessed | tf_op | source)
XLA Modules:
  0.0 199.3 jit_solution(724303152982355710)
XLA Ops:
  0.6 5.5 %cut_blocks.1 = bf16[16,2,3,48,384]{4,3,2,1,0:T(8,128)(2,1)} custom-call(bf16[3,768,768]{2,1,0:T(8,128)(2,1)} %bitcast.30), custom_call_target="tpu_custom_call" | custom-call | bytes 7077888 | tf_op jit(solution)/shard_map/cut_blocks/pallas_call | solution.py:267
  6.1 7.7 %all-to-all-start = ((bf16[32,3,48,384]{3,2,1,0:T(8,128)(2,1)}), bf16[32,3,48,384]{3,2,1,0:T(8,128)(2,1)S(1)}, u32[]{:S(2)}, u32[]{:S(2)}) async-start(bf16[32,3,48,384]{3,2,1,0:T(8,128)(2,1)} %bitcast.29), calls=%async_computation | async-start | bytes 7077888 | tf_op jit(solution)/shard_map/all_to_all | solution.py:420
  13.8 4.1 %collective-permute-start.5 = (bf16[192,3072]{1,0:T(8,128)(2,1)}, bf16[192,3072]{1,0:T(8,128)(2,1)}, u32[]{:S(2)}, u32[]{:S(2)}) collective-permute-start(bf16[192,3072]{1,0:T(8,128)(2,1)} %refs_0_.1), channel_id=1, source_target_pairs={{0,3},{1,0},{2,1},{3,2},{4,7},{5,4},{6,5},{7,6},{8,11},{9,8},{10,9... | collective-permute-start | bytes 3538952 | tf_op jit(solution)/shard_map/ppermute | solution.py:415
  17.9 0.0 collective-permute-start.4
  17.9 0.0 collective-permute-start
  17.9 0.1 select_reduce_fusion
  18.1 0.7 ne.200
  18.8 0.6 broadcast_divide_fusion
  19.4 0.8 div.99
  20.1 1.4 rem.317
  21.5 0.7 fusion
  22.3 0.7 add_add_fusion
  23.0 1.0 reshape.247
  24.0 0.0 collective-permute-done
  24.0 0.7 fusion.21
  24.7 2.1 %collective-permute-start.2 = (s32[2,6,128]{2,1,0:T(8,128)S(1)}, s32[2,6,128]{2,1,0:T(8,128)S(1)}, u32[]{:S(2)}, u32[]{:S(2)}) collective-permute-start(s32[2,6,128]{2,1,0:T(8,128)S(1)} %get-tuple-element.64), channel_id=1, source_target_pairs={{0,16},{8,24},{16,0},{24,8},{1,17},{9,25},{17,1},{25,9},{2,18},{10... | collective-permute-start | bytes 18440 | tf_op jit(solution)/shard_map/ppermute | solution.py:382
  26.7 0.0 collective-permute-start.1
  26.7 2.0 %collective-permute-start.3 = (s32[2,6,128]{2,1,0:T(8,128)S(1)}, s32[2,6,128]{2,1,0:T(8,128)S(1)}, u32[]{:S(2)}, u32[]{:S(2)}) collective-permute-start(s32[2,6,128]{2,1,0:T(8,128)S(1)} %get-tuple-element.64), channel_id=1, source_target_pairs={{0,24},{8,0},{16,8},{24,16},{1,25},{9,1},{17,9},{25,17},{2,26},{10... | collective-permute-start | bytes 18440 | tf_op jit(solution)/shard_map/ppermute | solution.py:382
  28.8 24.7 %collective-permute-done.2 = s32[2,6,128]{2,1,0:T(8,128)S(1)} collective-permute-done((s32[2,6,128]{2,1,0:T(8,128)S(1)}, s32[2,6,128]{2,1,0:T(8,128)S(1)}, u32[]{:S(2)}, u32[]{:S(2)}) %collective-permute-start.2) | collective-permute-done | bytes 6176 | tf_op jit(solution)/shard_map/ppermute | solution.py:382
  53.5 0.3 collective-permute-done.1
  53.8 0.0 collective-permute-done.3
  53.8 0.6 pad_add_fusion
  54.4 1.4 reshape.240
  55.8 3.1 %all-to-all-done = bf16[32,3,48,384]{3,2,1,0:T(8,128)(2,1)S(1)} async-done(((bf16[32,3,48,384]{3,2,1,0:T(8,128)(2,1)}), bf16[32,3,48,384]{3,2,1,0:T(8,128)(2,1)S(1)}, u32[]{:S(2)}, u32[]{:S(2)}) %all-to-all-start) | async-done | bytes 3538976 | tf_op jit(solution)/shard_map/all_to_all | solution.py:420
  58.8 3.6 %gather_fusion = bf16[576,8,384]{2,1,0:T(8,128)(2,1)} fusion(bf16[576,8,384]{2,1,0:T(8,128)(2,1)S(1)} %bitcast.28, s32[1024]{0:T(1024)S(1)} %pad_clamp_fusion), kind=kCustom, calls=%fused_computation | custom fusion | bytes 7080192 | tf_op jit(solution)/shard_map/jit(_take)/gather | solution.py:421
  62.4 0.0 collective-permute-done.5.refs_3_
  62.4 0.0 collective-permute-done.4.refs_1_
  62.4 6.0 %all-to-all-start.1 = ((bf16[32,3,48,384]{3,2,1,0:T(8,128)(2,1)}), bf16[32,3,48,384]{3,2,1,0:T(8,128)(2,1)S(1)}, u32[]{:S(2)}, u32[]{:S(2)}) async-start(bf16[32,3,48,384]{3,2,1,0:T(8,128)(2,1)} %bitcast.4), calls=%async_computation.1 | async-start | bytes 7077888 | tf_op jit(solution)/shard_map/all_to_all | solution.py:427
  68.5 4.0 %collective-permute-start.6 = (bf16[192,3072]{1,0:T(8,128)(2,1)}, bf16[192,3072]{1,0:T(8,128)(2,1)}, u32[]{:S(2)}, u32[]{:S(2)}) collective-permute-start(bf16[192,3072]{1,0:T(8,128)(2,1)} %refs_0_.1), channel_id=1, source_target_pairs={{0,2},{1,3},{2,0},{3,1},{4,6},{5,7},{6,4},{7,5},{8,10},{9,11},{10,... | collective-permute-start | bytes 3538952 | tf_op jit(solution)/shard_map/ppermute | solution.py:415
  72.4 0.1 compare_select_fusion.19
  72.5 0.1 iota_compare_fusion.3
  72.6 0.1 iota_compare_fusion.1
  72.7 1.6 select_reduce_fusion.1
  74.3 1.5 collective-permute-start.7
  75.7 2.7 %collective-permute-start.8 = (s32[6,128]{1,0:T(8,128)}, s32[6,128]{1,0:T(8,128)S(1)}, u32[]{:S(2)}, u32[]{:S(2)}) collective-permute-start(s32[6,128]{1,0:T(8,128)} %get-tuple-element.39), channel_id=1, source_target_pairs={{0,64},{32,96},{64,0},{96,32},{1,65},{33,97},{65,1},{97,33},{2,66}... | collective-permute-start | bytes 9224 | tf_op jit(solution)/shard_map/ppermute | solution.py:445
  78.5 1.4 collective-permute-start.9
  79.9 1.3 broadcast_in_dim.84.qg_ref
  81.1 1.3 broadcast_in_dim.85.kg_ref
  82.4 16.6 %collective-permute-done.6.refs_2_ = bf16[192,3072]{1,0:T(8,128)(2,1)} collective-permute-done((bf16[192,3072]{1,0:T(8,128)(2,1)}, bf16[192,3072]{1,0:T(8,128)(2,1)}, u32[]{:S(2)}, u32[]{:S(2)}) %collective-permute-start.6) | collective-permute-done | bytes 1179680 | tf_op jit(solution)/shard_map/ppermute | solution.py:415
  99.0 9.3 %grad_products.1 = (bf16[768,768]{1,0:T(8,128)(2,1)}, bf16[3072,768]{1,0:T(8,128)(2,1)}) custom-call(s32[1]{0:T(128)} %bitcast.here_ref, bf16[192,3072]{1,0:T(8,128)(2,1)} %refs_0_.1, bf16[192,3072]{1,0:T(8,128)(2,1)} %collective-permute-done.4.refs_1_, bf16[192,3072]{1,0:T(8,128)(2,1)} %collective-permute-done.6.refs_2_, ...), custom_call_target="tpu_custom_call" | custom-call | flops 1 | bytes 1 | tf_op jit(solution)/shard_map/grad_products/pallas_call | solution.py:315
  108.3 1.0 collective-permute-done.7
  109.3 4.3 %collective-permute-done.8 = s32[6,128]{1,0:T(8,128)S(1)} collective-permute-done((s32[6,128]{1,0:T(8,128)}, s32[6,128]{1,0:T(8,128)S(1)}, u32[]{:S(2)}, u32[]{:S(2)}) %collective-permute-start.8) | collective-permute-done | bytes 3104 | tf_op jit(solution)/shard_map/ppermute | solution.py:445
  113.6 0.0 collective-permute-done.9
  113.7 0.0 copy-start.4
  113.7 0.9 copy.13
  114.6 0.0 all-to-all-done.1
  114.6 1.8 copy-done
  116.4 19.6 %attention_forward.1 = (bf16[768,768]{1,0:T(8,128)(2,1)}, bf16[6,768,768]{2,1,0:T(8,128)(2,1)}, bf16[192,3072]{1,0:T(8,128)(2,1)}, bf16[192,3072]{1,0:T(8,128)(2...) custom-call(s32[1]{0:T(128)} %bitcast.here_ref, ...), custom_call_target="tpu_custom_call" | custom-call | flops 5435817984 | bytes 21233664 | tf_op jit(solution)/shard_map/attention_forward/pallas_call | solution.py:183
  136.0 2.2 %collective-permute-start.10 = (bf16[192,3072]{1,0:T(8,128)(2,1)}, bf16[192,3072]{1,0:T(8,128)(2,1)}, u32[]{:S(2)}, u32[]{:S(2)}) collective-permute-start(bf16[192,3072]{1,0:T(8,128)(2,1)} %get-tuple-element.42), channel_id=1, source_target_pairs={{0,1},{1,2},{2,3},{3,0},{4,5},{5,6},{6,7},{7,4},{8,9},{9,10},{10,1... | collective-permute-start | bytes 3538952 | tf_op jit(solution)/shard_map/ppermute | solution.py:455
  138.2 3.6 %collective-permute-start.11 = (bf16[192,3072]{1,0:T(8,128)(2,1)}, bf16[192,3072]{1,0:T(8,128)(2,1)}, u32[]{:S(2)}, u32[]{:S(2)}) collective-permute-start(bf16[192,3072]{1,0:T(8,128)(2,1)} %get-tuple-element.43), channel_id=1, source_target_pairs={{0,2},{1,3},{2,0},{3,1},{4,6},{5,7},{6,4},{7,5},{8,10},{9,11},{10,... | collective-permute-start | bytes 3538952 | tf_op jit(solution)/shard_map/ppermute | solution.py:455
  141.8 1.0 collective-permute-start.12
  142.8 4.8 %weight_terms.3 = bf16[16,96,768]{2,1,0:T(8,128)(2,1)} custom-call(s32[1]{0:T(128)} %bitcast.15.core_ref, bf16[16,2,96,768]{3,2,1,0:T(8,128)(2,1)} %bitcast.43, bf16[768,768]{1,0:T(8,128)(2,1)} %get-tuple-element.47.att_ref), custom_call_target="tpu_custom_call" | custom-call | flops 999999995904 | bytes 1000000000 | tf_op jit(solution)/shard_map/weight_terms/pallas_call | solution.py:354
  147.6 0.0 collective-permute-start.13
  147.6 4.9 %weight_terms.2 = bf16[16,96,768]{2,1,0:T(8,128)(2,1)} custom-call(s32[1]{0:T(128)} %bitcast.13.core_ref, bf16[16,2,96,768]{3,2,1,0:T(8,128)(2,1)} %bitcast.44, bf16[768,768]{1,0:T(8,128)(2,1)} %get-tuple-element.47.att_ref), custom_call_target="tpu_custom_call" | custom-call | flops 999999995904 | bytes 1000000000 | tf_op jit(solution)/shard_map/weight_terms/pallas_call | solution.py:354
  152.5 0.0 collective-permute-done.13
  152.5 4.5 %add_convert_fusion = bf16[16,96,768]{2,1,0:T(8,128)(2,1)} fusion(bf16[16,96,768]{2,1,0:T(8,128)(2,1)} %collective-permute-done.13, bf16[16,96,768]{2,1,0:T(8,128)(2,1)} %weight_terms.2), kind=kLoop, calls=%fused_computation.2 | loop fusion | flops 4718592 | bytes 7077888 | tf_op jit(solution)/shard_map/convert_element_type | solution.py:462
  157.0 5.8 %all-to-all-start.2 = ((bf16[16,96,768]{2,1,0:T(8,128)(2,1)}), bf16[16,96,768]{2,1,0:T(8,128)(2,1)}, u32[]{:S(2)}, u32[]{:S(2)}) async-start(bf16[16,96,768]{2,1,0:T(8,128)(2,1)} %add_convert_fusion), calls=%async_computation.2 | async-start | bytes 4718592 | tf_op jit(solution)/shard_map/all_to_all | solution.py:464
  162.8 14.4 %attention_backward.1 = bf16[3,768,768]{2,1,0:T(8,128)(2,1)} custom-call(bf16[16,2,3,48,384]{4,3,2,1,0:T(8,128)(2,1)} %bitcast.34, bf16[16,2,3,48,384]{4,3,2,1,0:T(8,128)(2,1)} %bitcast.35, bf16[16,2,3,48,384]{4,3,2,1,0:T(8,128)(2,1)} %bitcast.36, bf16[6,768,768]{2,1,0:T(8,128)(2,1)} %get-tuple-element.48.prob_ref, ...), custom_call_target="tpu_custom_call" | custom-call | flops 999999995904 | bytes 1000000000 | tf_op jit(solution)/shard_map/attention_backward/pallas_call | solution.py:237
  177.2 0.0 collective-permute-done.10
  177.2 15.6 %collective-permute-done.11 = bf16[192,3072]{1,0:T(8,128)(2,1)} collective-permute-done((bf16[192,3072]{1,0:T(8,128)(2,1)}, bf16[192,3072]{1,0:T(8,128)(2,1)}, u32[]{:S(2)}, u32[]{:S(2)}) %collective-permute-start.11) | collective-permute-done | bytes 1179680 | tf_op jit(solution)/shard_map/ppermute | solution.py:455
  192.9 0.0 collective-permute-done.12
  192.9 3.7 %add_convert_fusion.1 = bf16[192,3072]{1,0:T(8,128)(2,1)} fusion(bf16[192,3072]{1,0:T(8,128)(2,1)} %collective-permute-done.12, bf16[192,3072]{1,0:T(8,128)(2,1)} %collective-permute-done.11, bf16[192,3072]{1,0:T(8,128)(2,1)} %collective-permute-done.10, bf16[192,3072]{1,0:T(8,128)(2,1)S(1)} %copy-done.1), kind=kLoop, calls=%fused_computation.3 | loop fusion | flops 4718592 | bytes 5898240 | tf_op jit(solution)/shard_map/convert_element_type | solution.py:467
  196.6 0.0 all-to-all-done.2
  196.6 2.7 %convert_reduce_fusion = f32[96,768]{1,0:T(8,128)} fusion(bf16[16,96,768]{2,1,0:T(8,128)(2,1)} %all-to-all-done.2), kind=kLoop, calls=%fused_computation.1 | loop fusion | flops 2285568 | bytes 2654208 | tf_op jit(solution)/shard_map/reduce_sum | solution.py:468
  (15 shorter events, 0.0 us)
Async XLA Ops:
  6.1 11.8 %copy-start.5 = (s32[192]{0:T(256)S(1)}, s32[192]{0:T(256)}, u32[]{:S(2)}) copy-start(s32[192]{0:T(256)} %param.9) | copy-start | bytes 2308
  6.1 52.7 %all-to-all-start = ((bf16[32,3,48,384]{3,2,1,0:T(8,128)(2,1)}), bf16[32,3,48,384]{3,2,1,0:T(8,128)(2,1)S(1)}, u32[]{:S(2)}, u32[]{:S(2)}) async-start(bf16[32,3,48,384]{3,2,1,0:T(8,128)(2,1)} %bitcast.29), calls=%async_computation | async-start | bytes 7077888 | tf_op jit(solution)/shard_map/all_to_all | solution.py:420
  13.8 48.6 %collective-permute-start.5 = (bf16[192,3072]{1,0:T(8,128)(2,1)}, bf16[192,3072]{1,0:T(8,128)(2,1)}, u32[]{:S(2)}, u32[]{:S(2)}) collective-permute-start(bf16[192,3072]{1,0:T(8,128)(2,1)} %refs_0_.1), channel_id=1, source_target_pairs={{0,3},{1,0},{2,1},{3,2},{4,7},{5,4},{6,5},{7,6},{8,11},{9,8},{10,9... | collective-permute-start | bytes 3538952 | tf_op jit(solution)/shard_map/ppermute | solution.py:415
  17.9 44.5 %collective-permute-start.4 = (bf16[192,3072]{1,0:T(8,128)(2,1)}, bf16[192,3072]{1,0:T(8,128)(2,1)}, u32[]{:S(2)}, u32[]{:S(2)}) collective-permute-start(bf16[192,3072]{1,0:T(8,128)(2,1)} %refs_0_.1), channel_id=1, source_target_pairs={{0,1},{1,2},{2,3},{3,0},{4,5},{5,6},{6,7},{7,4},{8,9},{9,10},{10,1... | collective-permute-start | bytes 3538952 | tf_op jit(solution)/shard_map/ppermute | solution.py:415
  17.9 6.0 %collective-permute-start = (s32[6,128]{1,0:T(8,128)}, s32[6,128]{1,0:T(8,128)}, u32[]{:S(2)}, u32[]{:S(2)}) collective-permute-start(s32[6,128]{1,0:T(8,128)} %bitcast.6), channel_id=1, source_target_pairs={{0,4},{4,0},{1,5},{5,1},{2,6},{6,2},{3,7},{7,3},{8,12},{12,8},{9,1... | collective-permute-start | bytes 9224 | tf_op jit(solution)/shard_map/ppermute | solution.py:382
  18.0 1.3 copy-start.2
  24.7 28.8 %collective-permute-start.2 = (s32[2,6,128]{2,1,0:T(8,128)S(1)}, s32[2,6,128]{2,1,0:T(8,128)S(1)}, u32[]{:S(2)}, u32[]{:S(2)}) collective-permute-start(s32[2,6,128]{2,1,0:T(8,128)S(1)} %get-tuple-element.64), channel_id=1, source_target_pairs={{0,16},{8,24},{16,0},{24,8},{1,17},{9,25},{17,1},{25,9},{2,18},{10... | collective-permute-start | bytes 18440 | tf_op jit(solution)/shard_map/ppermute | solution.py:382
  26.7 27.0 %collective-permute-start.1 = (s32[2,6,128]{2,1,0:T(8,128)S(1)}, s32[2,6,128]{2,1,0:T(8,128)S(1)}, u32[]{:S(2)}, u32[]{:S(2)}) collective-permute-start(s32[2,6,128]{2,1,0:T(8,128)S(1)} %get-tuple-element.64), channel_id=1, source_target_pairs={{0,8},{8,16},{16,24},{24,0},{1,9},{9,17},{17,25},{25,1},{2,10},{10... | collective-permute-start | bytes 18440 | tf_op jit(solution)/shard_map/ppermute | solution.py:382
  26.7 27.0 %collective-permute-start.3 = (s32[2,6,128]{2,1,0:T(8,128)S(1)}, s32[2,6,128]{2,1,0:T(8,128)S(1)}, u32[]{:S(2)}, u32[]{:S(2)}) collective-permute-start(s32[2,6,128]{2,1,0:T(8,128)S(1)} %get-tuple-element.64), channel_id=1, source_target_pairs={{0,24},{8,0},{16,8},{24,16},{1,25},{9,1},{17,9},{25,17},{2,26},{10... | collective-permute-start | bytes 18440 | tf_op jit(solution)/shard_map/ppermute | solution.py:382
  62.4 10.0 %copy-start.3 = (s32[192]{0:T(256)S(1)}, s32[192]{0:T(256)}, u32[]{:S(2)}) copy-start(s32[192]{0:T(256)} %copy-done.2) | copy-start | bytes 2308
  62.4 52.2 %all-to-all-start.1 = ((bf16[32,3,48,384]{3,2,1,0:T(8,128)(2,1)}), bf16[32,3,48,384]{3,2,1,0:T(8,128)(2,1)S(1)}, u32[]{:S(2)}, u32[]{:S(2)}) async-start(bf16[32,3,48,384]{3,2,1,0:T(8,128)(2,1)} %bitcast.4), calls=%async_computation.1 | async-start | bytes 7077888 | tf_op jit(solution)/shard_map/all_to_all | solution.py:427
  68.5 30.6 %collective-permute-start.6 = (bf16[192,3072]{1,0:T(8,128)(2,1)}, bf16[192,3072]{1,0:T(8,128)(2,1)}, u32[]{:S(2)}, u32[]{:S(2)}) collective-permute-start(bf16[192,3072]{1,0:T(8,128)(2,1)} %refs_0_.1), channel_id=1, source_target_pairs={{0,2},{1,3},{2,0},{3,1},{4,6},{5,7},{6,4},{7,5},{8,10},{9,11},{10,... | collective-permute-start | bytes 3538952 | tf_op jit(solution)/shard_map/ppermute | solution.py:415
  74.3 35.1 %collective-permute-start.7 = (s32[6,128]{1,0:T(8,128)}, s32[6,128]{1,0:T(8,128)S(1)}, u32[]{:S(2)}, u32[]{:S(2)}) collective-permute-start(s32[6,128]{1,0:T(8,128)} %get-tuple-element.38), channel_id=1, source_target_pairs={{0,32},{32,64},{64,96},{96,0},{1,33},{33,65},{65,97},{97,1},{2,34}... | collective-permute-start | bytes 9224 | tf_op jit(solution)/shard_map/ppermute | solution.py:445
  75.7 37.9 %collective-permute-start.8 = (s32[6,128]{1,0:T(8,128)}, s32[6,128]{1,0:T(8,128)S(1)}, u32[]{:S(2)}, u32[]{:S(2)}) collective-permute-start(s32[6,128]{1,0:T(8,128)} %get-tuple-element.39), channel_id=1, source_target_pairs={{0,64},{32,96},{64,0},{96,32},{1,65},{33,97},{65,1},{97,33},{2,66}... | collective-permute-start | bytes 9224 | tf_op jit(solution)/shard_map/ppermute | solution.py:445
  78.5 35.2 %collective-permute-start.9 = (s32[6,128]{1,0:T(8,128)}, s32[6,128]{1,0:T(8,128)S(1)}, u32[]{:S(2)}, u32[]{:S(2)}) collective-permute-start(s32[6,128]{1,0:T(8,128)} %get-tuple-element.40), channel_id=1, source_target_pairs={{0,96},{32,0},{64,32},{96,64},{1,97},{33,1},{65,33},{97,65},{2,98}... | collective-permute-start | bytes 9224 | tf_op jit(solution)/shard_map/ppermute | solution.py:445
  113.7 1.0 copy-start.4
  114.6 1.8 copy-start
  136.0 41.2 %collective-permute-start.10 = (bf16[192,3072]{1,0:T(8,128)(2,1)}, bf16[192,3072]{1,0:T(8,128)(2,1)}, u32[]{:S(2)}, u32[]{:S(2)}) collective-permute-start(bf16[192,3072]{1,0:T(8,128)(2,1)} %get-tuple-element.42), channel_id=1, source_target_pairs={{0,1},{1,2},{2,3},{3,0},{4,5},{5,6},{6,7},{7,4},{8,9},{9,10},{10,1... | collective-permute-start | bytes 3538952 | tf_op jit(solution)/shard_map/ppermute | solution.py:455
  138.2 54.7 %collective-permute-start.11 = (bf16[192,3072]{1,0:T(8,128)(2,1)}, bf16[192,3072]{1,0:T(8,128)(2,1)}, u32[]{:S(2)}, u32[]{:S(2)}) collective-permute-start(bf16[192,3072]{1,0:T(8,128)(2,1)} %get-tuple-element.43), channel_id=1, source_target_pairs={{0,2},{1,3},{2,0},{3,1},{4,6},{5,7},{6,4},{7,5},{8,10},{9,11},{10,... | collective-permute-start | bytes 3538952 | tf_op jit(solution)/shard_map/ppermute | solution.py:455
  141.8 51.1 %collective-permute-start.12 = (bf16[192,3072]{1,0:T(8,128)(2,1)}, bf16[192,3072]{1,0:T(8,128)(2,1)}, u32[]{:S(2)}, u32[]{:S(2)}) collective-permute-start(bf16[192,3072]{1,0:T(8,128)(2,1)} %get-tuple-element.44), channel_id=1, source_target_pairs={{0,3},{1,0},{2,1},{3,2},{4,7},{5,4},{6,5},{7,6},{8,11},{9,8},{10,9... | collective-permute-start | bytes 3538952 | tf_op jit(solution)/shard_map/ppermute | solution.py:455
  147.6 4.9 %collective-permute-start.13 = (bf16[16,96,768]{2,1,0:T(8,128)(2,1)}, bf16[16,96,768]{2,1,0:T(8,128)(2,1)}, u32[]{:S(2)}, u32[]{:S(2)}) collective-permute-start(bf16[16,96,768]{2,1,0:T(8,128)(2,1)} %weight_terms.3), channel_id=1, source_target_pairs={{0,4},{4,0},{1,5},{5,1},{2,6},{6,2},{3,7},{7,3},{8,12},{12,8},{9,1... | collective-permute-start | bytes 7077896 | tf_op jit(solution)/shard_map/ppermute | solution.py:460
  157.0 39.7 %all-to-all-start.2 = ((bf16[16,96,768]{2,1,0:T(8,128)(2,1)}), bf16[16,96,768]{2,1,0:T(8,128)(2,1)}, u32[]{:S(2)}, u32[]{:S(2)}) async-start(bf16[16,96,768]{2,1,0:T(8,128)(2,1)} %add_convert_fusion), calls=%async_computation.2 | async-start | bytes 4718592 | tf_op jit(solution)/shard_map/all_to_all | solution.py:464
  162.8 30.1 %copy-start.1 = (bf16[192,3072]{1,0:T(8,128)(2,1)S(1)}, bf16[192,3072]{1,0:T(8,128)(2,1)}, u32[]{:S(2)}) copy-start(bf16[192,3072]{1,0:T(8,128)(2,1)} %get-tuple-element.51) | copy-start | bytes 3538948

commit v2 on v1

--- a/solution.py
+++ b/solution.py
@@ -21,6 +21,8 @@
 FORWARD_HEADS = 3
 BACKWARD_ROWS = 768
 VMEM_LIMIT = 56 * 1024 * 1024
+FORWARD_VMEM = 50 * 1024 * 1024
+WEIGHT_VMEM = 40 * 1024 * 1024
 LITTLE = pl.CostEstimate(flops=1, bytes_accessed=1, transcendentals=0)
 LARGE = pl.CostEstimate(flops=10**12, bytes_accessed=10**9, transcendentals=0)
 
@@ -209,7 +211,7 @@
         ]
         + [jax.ShapeDtypeStruct((share, d_out), jnp.bfloat16)] * places
         + [jax.ShapeDtypeStruct((rows, heads * HD), jnp.bfloat16)],
-        compiler_params=pltpu.CompilerParams(vmem_limit_bytes=VMEM_LIMIT),
+        compiler_params=pltpu.CompilerParams(vmem_limit_bytes=FORWARD_VMEM),
         cost_estimate=pl.CostEstimate(
             flops=4 * heads * rows * rows * HD + 2 * rows * d_out * heads * HD,
             bytes_accessed=2 * heads * rows * (rows + 4 * HD) + 4 * rows * d_out,
@@ -254,11 +256,13 @@
 
 
 def cut_kernel(rows_ref, out_ref):
-    cuts, span = out_ref.shape[0], out_ref.shape[3]
+    cuts, sides, _, span, half = out_ref.shape
     rows8 = BLK // cuts
-    tiles = rows_ref[0].astype(jnp.float32).reshape(span // rows8, cuts, rows8, -1)
+    tiles = rows_ref[0].astype(jnp.float32).reshape(span // rows8, cuts, rows8, sides * half)
     for cut in range(cuts):
-        out_ref[cut, 0, 0] = tiles[:, cut].reshape(span, -1).astype(jnp.bfloat16)
+        rows = tiles[:, cut].reshape(span, sides * half).astype(jnp.bfloat16)
+        for side in range(sides):
+            out_ref[cut, side, 0] = rows[:, side * half : (side + 1) * half]
 
 
 def cut_blocks(planes, cuts):
@@ -266,11 +270,9 @@
     span, half = rows // cuts, width // 2
     return pl.pallas_call(
         cut_kernel,
-        grid=(parts, 2),
-        in_specs=[pl.BlockSpec((1, rows, half), lambda part, side: (part, 0, side))],
-        out_specs=pl.BlockSpec(
-            (cuts, 1, 1, span, half), lambda part, side: (0, side, part, 0, 0)
-        ),
+        grid=(parts,),
+        in_specs=[pl.BlockSpec((1, rows, width), lambda part: (part, 0, 0))],
+        out_specs=pl.BlockSpec((cuts, 2, 1, span, half), lambda part: (0, 0, part, 0, 0)),
         out_shape=jax.ShapeDtypeStruct((cuts, 2, parts, span, half), jnp.bfloat16),
         compiler_params=pltpu.CompilerParams(vmem_limit_bytes=VMEM_LIMIT),
         cost_estimate=pl.CostEstimate(
@@ -363,7 +365,7 @@
             out_specs=block,
         ),
         out_shape=jax.ShapeDtypeStruct((peers // 2, share, width), jnp.bfloat16),
-        compiler_params=pltpu.CompilerParams(vmem_limit_bytes=VMEM_LIMIT),
+        compiler_params=pltpu.CompilerParams(vmem_limit_bytes=WEIGHT_VMEM),
         cost_estimate=LARGE,
         name="weight_terms",
     )(
@@ -451,15 +453,18 @@
     attended, probs, *partials, attended_back = attention_forward(
         landed, segments, q_gain, k_gain, out_weight, here, places
     )
-    partials = [partials[0]] + [
-        lax.ppermute(partials[by], "mp", turn(places, by)) for by in range(1, places)
-    ]
+    opposite = places // 2
+    for by in range(1, places):
+        if by != opposite:
+            partials[by] = lax.ppermute(partials[by], "mp", turn(places, by))
 
     core = lax.axis_index("core")
     given = weight_terms(1 - core, grad_columns, attended_back, peers)
     taken = lax.ppermute(given, "core", turn(2, 1))
     kept = weight_terms(core, grad_columns, attended_back, peers)
     pair = (kept.astype(jnp.float32) + taken.astype(jnp.float32)).astype(jnp.bfloat16)
+    pair, partials[opposite] = lax.optimization_barrier((pair, partials[opposite]))
+    partials[opposite] = lax.ppermute(partials[opposite], "mp", turn(places, opposite))
     probs, pair = lax.optimization_barrier((probs, pair))
     terms = lax.all_to_all(pair, ("x", "y"), split_axis=0, concat_axis=0, tiled=True)
     planes_grad = attention_backward(landed, probs, out_grad, attended, q_gain, k_gain)

time: 200 us -> 197 us (0.985)
  waiting for transfers between devices: 65.6 us -> 72.4 us
  Pallas kernels: 58.5 us -> 53.2 us
  local copies, waits for them, and re-layouts: 14.1 us -> 11.4 us
  other arithmetic: 16.3 us -> 14.3 us
    pallas_call x2, Pallas kernels: 9.71 us -> 5.74 us  [weight_terms(): pl.pallas_call(weight_kernel, grid_spec=pltpu.PrefetchScalarGridSpec(num_...]
    ppermute x3, waiting for transfers between devices: 16.6 us -> 20 us  [body(): lax.ppermute(cotangent, 'mp', turn(places, by))]
    ppermute x1, waiting for transfers between devices: 0.01 us -> 2.5 us  [body(): taken = lax.ppermute(given, 'core', turn(2, 1))]
  transfers between devices with their start and end apart: 17 -> 17, of which waited for: 7 -> 9; matrix products, arithmetic and copies ran while one was open for 13% -> 11% of each run, Pallas kernels for 17% -> 15%
where the time goes in v2:
time: 197 us; the launch traced here: 196 us
  waiting for transfers between devices  72.4 us (37%)
  Pallas kernels  53.2 us (27%)
  starting transfers between devices  43.7 us (22%)
  other arithmetic  14.3 us (7%)
  local copies, waits for them, and re-layouts  11.4 us (6%)
    ppermute x4, waiting for transfers between devices, gathered(): lax.ppermute(own, axis, turn(size, by))  25 us
    ppermute x3, waiting for transfers between devices, body(): lax.ppermute(cotangent, 'mp', turn(places, by))  20 us
    pallas_call x1, Pallas kernels, attention_forward(): pl.pallas_call(functools.partial(forward_kernel, groups), grid_spec=pltpu...  19.1 us
    ppermute x2, waiting for transfers between devices, body(): partials[by] = lax.ppermute(partials[by], 'mp', turn(places, by))  15.4 us
    pallas_call x1, Pallas kernels, attention_backward(): pl.pallas_call(functools.partial(backward_kernel, BACKWARD_ROWS), grid=(h...  14.3 us
    pallas_call x1, Pallas kernels, grad_products(): pl.pallas_call(grad_kernel, grid_spec=pltpu.PrefetchScalarGridSpec(num_sc...  9.31 us
    ppermute x3, starting transfers between devices, body(): lax.ppermute(cotangent, 'mp', turn(places, by))  8.06 us
    all_to_all x1, starting transfers between devices, body(): spread = lax.all_to_all(pieces, DP, split_axis=0, concat_axis=0, tiled=True)  7.67 us
  transfers between devices with their start and end apart: 17, of which 9 were waited for; matrix products, arithmetic and copies ran while one was open for 11% of the time, Pallas kernels for 15%

profile of v2, /device:TPU:8, one launch (start us, length us, event | category | flops | bytes accessed | tf_op | source)
XLA Modules:
  0.0 195.8 jit_solution(8456227186380836935)
XLA Ops:
  0.6 4.7 %cut_blocks.1 = bf16[16,2,3,48,384]{4,3,2,1,0:T(8,128)(2,1)} custom-call(bf16[3,768,768]{2,1,0:T(8,128)(2,1)} %bitcast.35), custom_call_target="tpu_custom_call" | custom-call | bytes 7077888 | tf_op jit(solution)/shard_map/cut_blocks/pallas_call | solution.py:271
  5.3 7.7 %all-to-all-start = ((bf16[32,3,48,384]{3,2,1,0:T(8,128)(2,1)}), bf16[32,3,48,384]{3,2,1,0:T(8,128)(2,1)S(1)}, u32[]{:S(2)}, u32[]{:S(2)}) async-start(bf16[32,3,48,384]{3,2,1,0:T(8,128)(2,1)} %bitcast.34), calls=%async_computation | async-start | bytes 7077888 | tf_op jit(solution)/shard_map/all_to_all | solution.py:422
  13.0 4.1 %collective-permute-start.5 = (bf16[192,3072]{1,0:T(8,128)(2,1)}, bf16[192,3072]{1,0:T(8,128)(2,1)}, u32[]{:S(2)}, u32[]{:S(2)}) collective-permute-start(bf16[192,3072]{1,0:T(8,128)(2,1)} %refs_0_.1), channel_id=1, source_target_pairs={{0,3},{1,0},{2,1},{3,2},{4,7},{5,4},{6,5},{7,6},{8,11},{9,8},{10,9... | collective-permute-start | bytes 3538952 | tf_op jit(solution)/shard_map/ppermute | solution.py:417
  17.1 0.0 collective-permute-start.4
  17.1 0.0 collective-permute-start
  17.1 0.1 select_reduce_fusion
  17.3 0.7 ne.200
  18.0 0.6 broadcast_divide_fusion
  18.6 0.8 div.99
  19.4 1.4 rem.317
  20.7 0.7 fusion
  21.5 0.7 add_add_fusion
  22.2 1.0 reshape.247
  23.2 0.0 collective-permute-done
  23.2 0.7 fusion.21
  23.9 2.1 %collective-permute-start.2 = (s32[2,6,128]{2,1,0:T(8,128)S(1)}, s32[2,6,128]{2,1,0:T(8,128)S(1)}, u32[]{:S(2)}, u32[]{:S(2)}) collective-permute-start(s32[2,6,128]{2,1,0:T(8,128)S(1)} %get-tuple-element.68), channel_id=1, source_target_pairs={{0,16},{8,24},{16,0},{24,8},{1,17},{9,25},{17,1},{25,9},{2,18},{10... | collective-permute-start | bytes 18440 | tf_op jit(solution)/shard_map/ppermute | solution.py:384
  26.0 0.0 collective-permute-start.1
  26.0 2.0 %collective-permute-start.3 = (s32[2,6,128]{2,1,0:T(8,128)S(1)}, s32[2,6,128]{2,1,0:T(8,128)S(1)}, u32[]{:S(2)}, u32[]{:S(2)}) collective-permute-start(s32[2,6,128]{2,1,0:T(8,128)S(1)} %get-tuple-element.68), channel_id=1, source_target_pairs={{0,24},{8,0},{16,8},{24,16},{1,25},{9,1},{17,9},{25,17},{2,26},{10... | collective-permute-start | bytes 18440 | tf_op jit(solution)/shard_map/ppermute | solution.py:384
  28.0 24.7 %collective-permute-done.2 = s32[2,6,128]{2,1,0:T(8,128)S(1)} collective-permute-done((s32[2,6,128]{2,1,0:T(8,128)S(1)}, s32[2,6,128]{2,1,0:T(8,128)S(1)}, u32[]{:S(2)}, u32[]{:S(2)}) %collective-permute-start.2) | collective-permute-done | bytes 6176 | tf_op jit(solution)/shard_map/ppermute | solution.py:384
  52.7 0.3 collective-permute-done.1
  53.0 0.0 collective-permute-done.3
  53.0 0.6 pad_add_fusion
  53.6 1.4 reshape.240
  54.9 3.1 %all-to-all-done = bf16[32,3,48,384]{3,2,1,0:T(8,128)(2,1)S(1)} async-done(((bf16[32,3,48,384]{3,2,1,0:T(8,128)(2,1)}), bf16[32,3,48,384]{3,2,1,0:T(8,128)(2,1)S(1)}, u32[]{:S(2)}, u32[]{:S(2)}) %all-to-all-start) | async-done | bytes 3538976 | tf_op jit(solution)/shard_map/all_to_all | solution.py:422
  58.0 3.6 %gather_fusion = bf16[576,8,384]{2,1,0:T(8,128)(2,1)} fusion(bf16[576,8,384]{2,1,0:T(8,128)(2,1)S(1)} %bitcast.33, s32[1024]{0:T(1024)S(1)} %pad_clamp_fusion), kind=kCustom, calls=%fused_computation | custom fusion | bytes 7080192 | tf_op jit(solution)/shard_map/jit(_take)/gather | solution.py:423
  61.6 0.0 collective-permute-done.5.refs_3_
  61.6 0.0 collective-permute-done.4.refs_1_
  61.6 0.0 copy-start.7
  61.7 0.0 copy-start.10
  61.7 0.0 copy-start.11
  61.7 6.2 %all-to-all-start.1 = ((bf16[32,3,48,384]{3,2,1,0:T(8,128)(2,1)}), bf16[32,3,48,384]{3,2,1,0:T(8,128)(2,1)}, u32[]{:S(2)}, u32[]{:S(2)}) async-start(bf16[32,3,48,384]{3,2,1,0:T(8,128)(2,1)} %bitcast.4), calls=%async_computation.1 | async-start | bytes 7077888 | tf_op jit(solution)/shard_map/all_to_all | solution.py:429
  67.9 4.0 %collective-permute-start.6 = (bf16[192,3072]{1,0:T(8,128)(2,1)S(1)}, bf16[192,3072]{1,0:T(8,128)(2,1)S(1)}, u32[]{:S(2)}, u32[]{:S(2)}) collective-permute-start(bf16[192,3072]{1,0:T(8,128)(2,1)S(1)} %copy-done.5), channel_id=1, source_target_pairs={{0,2},{1,3},{2,0},{3,1},{4,6},{5,7},{6,4},{7,5},{8,10},{9,11},{10,... | collective-permute-start | bytes 3538952 | tf_op jit(solution)/shard_map/ppermute | solution.py:417
  71.8 0.1 compare_select_fusion.19
  72.0 0.1 iota_compare_fusion.3
  72.1 0.1 iota_compare_fusion.1
  72.1 0.2 select_reduce_fusion.1
  72.4 1.5 collective-permute-start.7
  73.9 2.7 %collective-permute-start.8 = (s32[6,128]{1,0:T(8,128)S(1)}, s32[6,128]{1,0:T(8,128)S(1)}, u32[]{:S(2)}, u32[]{:S(2)}) collective-permute-start(s32[6,128]{1,0:T(8,128)S(1)} %get-tuple-element.41), channel_id=1, source_target_pairs={{0,64},{32,96},{64,0},{96,32},{1,65},{33,97},{65,1},{97,33},{2,66}... | collective-permute-start | bytes 9224 | tf_op jit(solution)/shard_map/ppermute | solution.py:447
  76.6 1.4 collective-permute-start.9
  78.1 0.0 copy-start
  78.1 20.0 %collective-permute-done.6.refs_2_ = bf16[192,3072]{1,0:T(8,128)(2,1)S(1)} collective-permute-done((bf16[192,3072]{1,0:T(8,128)(2,1)S(1)}, bf16[192,3072]{1,0:T(8,128)(2,1)S(1)}, u32[]{:S(2)}, u32[]{:S(2)}) %collective-permute-start.6) | collective-permute-done | bytes 1179680 | tf_op jit(solution)/shard_map/ppermute | solution.py:417
  98.1 1.0 copy-done.6
  99.1 9.3 %grad_products.1 = (bf16[768,768]{1,0:T(8,128)(2,1)}, bf16[3072,768]{1,0:T(8,128)(2,1)}) custom-call(s32[1]{0:T(128)} %bitcast.here_ref, bf16[192,3072]{1,0:T(8,128)(2,1)} %refs_0_.1, bf16[192,3072]{1,0:T(8,128)(2,1)} %collective-permute-done.4.refs_1_, bf16[192,3072]{1,0:T(8,128)(2,1)} %copy-done.6, bf16[192,3072]{1,0:T(8,128)(2,1)} %collective-permute-done.5.refs_3_, ...), custom_call_target="tpu_custom_call" | custom-call | flops 1 | bytes 1 | tf_op jit(solution)/shard_map/grad_products/pallas_call | solution.py:317
  108.4 0.3 collective-permute-done.7
  108.7 4.3 %collective-permute-done.8 = s32[6,128]{1,0:T(8,128)S(1)} collective-permute-done((s32[6,128]{1,0:T(8,128)S(1)}, s32[6,128]{1,0:T(8,128)S(1)}, u32[]{:S(2)}, u32[]{:S(2)}) %collective-permute-start.8) | collective-permute-done | bytes 3104 | tf_op jit(solution)/shard_map/ppermute | solution.py:447
  113.0 0.0 collective-permute-done.9
  113.0 0.2 copy.13
  113.2 0.0 all-to-all-done.1
  113.3 19.1 %attention_forward.1 = (bf16[768,768]{1,0:T(8,128)(2,1)S(1)}, bf16[6,768,768]{2,1,0:T(8,128)(2,1)}, bf16[192,3072]{1,0:T(8,128)(2,1)S(1)}, bf16[192,3072]{1,0:T(...) custom-call(s32[1]{0:T(128)} %bitcast.here_ref, ...), custom_call_target="tpu_custom_call" | custom-call | flops 5435817984 | bytes 21233664 | tf_op jit(solution)/shard_map/attention_forward/pallas_call | solution.py:185
  132.4 2.2 %collective-permute-start.10 = (bf16[192,3072]{1,0:T(8,128)(2,1)}, bf16[192,3072]{1,0:T(8,128)(2,1)}, u32[]{:S(2)}, u32[]{:S(2)}) collective-permute-start(bf16[192,3072]{1,0:T(8,128)(2,1)} %get-tuple-element.44), channel_id=1, source_target_pairs={{0,1},{1,2},{2,3},{3,0},{4,5},{5,6},{6,7},{7,4},{8,9},{9,10},{10,1... | collective-permute-start | bytes 3538952 | tf_op jit(solution)/shard_map/ppermute | solution.py:459
  134.6 2.2 %collective-permute-start.13 = (bf16[192,3072]{1,0:T(8,128)(2,1)}, bf16[192,3072]{1,0:T(8,128)(2,1)}, u32[]{:S(2)}, u32[]{:S(2)}) collective-permute-start(bf16[192,3072]{1,0:T(8,128)(2,1)} %get-tuple-element.49), channel_id=1, source_target_pairs={{0,3},{1,0},{2,1},{3,2},{4,7},{5,4},{6,5},{7,6},{8,11},{9,8},{10,9... | collective-permute-start | bytes 3538952 | tf_op jit(solution)/shard_map/ppermute | solution.py:459
  136.8 1.3 copy-done.4
  138.1 3.4 %weight_terms.3 = bf16[16,96,768]{2,1,0:T(8,128)(2,1)} custom-call(s32[1]{0:T(128)} %bitcast.15.core_ref, bf16[16,2,96,768]{3,2,1,0:T(8,128)(2,1)S(1)} %bitcast.31, bf16[768,768]{1,0:T(8,128)(2,1)S(1)} %copy-done.4), custom_call_target="tpu_custom_call" | custom-call | flops 999999995904 | bytes 1000000000 | tf_op jit(solution)/shard_map/weight_terms/pallas_call | solution.py:356
  141.4 0.0 collective-permute-start.11
  141.4 2.4 %weight_terms.2 = bf16[16,96,768]{2,1,0:T(8,128)(2,1)S(1)} custom-call(s32[1]{0:T(128)} %bitcast.13.core_ref, bf16[16,2,96,768]{3,2,1,0:T(8,128)(2,1)S(1)} %bitcast.32, bf16[768,768]{1,0:T(8,128)(2,1)S(1)} %copy-done.4), custom_call_target="tpu_custom_call" | custom-call | flops 999999995904 | bytes 1000000000 | tf_op jit(solution)/shard_map/weight_terms/pallas_call | solution.py:356
  143.8 2.5 %collective-permute-done.11 = bf16[16,96,768]{2,1,0:T(8,128)(2,1)} collective-permute-done((bf16[16,96,768]{2,1,0:T(8,128)(2,1)}, bf16[16,96,768]{2,1,0:T(8,128)(2,1)}, u32[]{:S(2)}, u32[]{:S(2)}) %collective-permute-start.11) | collective-permute-done | bytes 2359328 | tf_op jit(solution)/shard_map/ppermute | solution.py:463
  146.3 3.8 %add_convert_fusion = bf16[16,96,768]{2,1,0:T(8,128)(2,1)} fusion(bf16[16,96,768]{2,1,0:T(8,128)(2,1)} %collective-permute-done.11, bf16[16,96,768]{2,1,0:T(8,128)(2,1)S(1)} %weight_terms.2), kind=kLoop, calls=%fused_computation.2 | loop fusion | flops 4718592 | bytes 7077888 | tf_op jit(solution)/shard_map/convert_element_type | solution.py:465
  150.1 5.8 %all-to-all-start.2 = ((bf16[16,96,768]{2,1,0:T(8,128)(2,1)}), bf16[16,96,768]{2,1,0:T(8,128)(2,1)}, u32[]{:S(2)}, u32[]{:S(2)}) async-start(bf16[16,96,768]{2,1,0:T(8,128)(2,1)} %add_convert_fusion), calls=%async_computation.2 | async-start | bytes 4718592 | tf_op jit(solution)/shard_map/all_to_all | solution.py:469
  156.0 1.8 collective-permute-start.12
  157.8 14.3 %attention_backward.1 = bf16[3,768,768]{2,1,0:T(8,128)(2,1)} custom-call(bf16[16,2,3,48,384]{4,3,2,1,0:T(8,128)(2,1)} %bitcast.12.q_ref.k_ref.v_ref, bf16[16,2,3,48,384]{4,3,2,1,0:T(8,128)(2,1)} %bitcast.12.q_ref.k_ref.v_ref, bf16[16,2,3,48,384]{4,3,2,1,0:T(8,128)(2,1)} %bitcast.12.q_ref.k_ref.v_ref, bf16[6,768,768]{2,1,0:T(8,128)(2,1)} %get-tuple-element.52.prob_ref, ...), custom_call_target="tpu_custom_call" | custom-call | flops 999999995904 | bytes 1000000000 | tf_op jit(solution)/shard_map/attention_backward/pallas_call | solution.py:239
  172.1 15.4 %collective-permute-done.13 = bf16[192,3072]{1,0:T(8,128)(2,1)} collective-permute-done((bf16[192,3072]{1,0:T(8,128)(2,1)}, bf16[192,3072]{1,0:T(8,128)(2,1)}, u32[]{:S(2)}, u32[]{:S(2)}) %collective-permute-start.13) | collective-permute-done | bytes 1179680 | tf_op jit(solution)/shard_map/ppermute | solution.py:459
  187.5 1.8 collective-permute-done.12
  189.3 3.7 %add_convert_fusion.1 = bf16[192,3072]{1,0:T(8,128)(2,1)} fusion(bf16[192,3072]{1,0:T(8,128)(2,1)} %collective-permute-done.13, bf16[192,3072]{1,0:T(8,128)(2,1)} %collective-permute-done.12, bf16[192,3072]{1,0:T(8,128)(2,1)} %collective-permute-done.10, bf16[192,3072]{1,0:T(8,128)(2,1)S(1)} %get-tuple-element.55), kind=kLoop, calls=%fused_computation.3 | loop fusion | flops 4718592 | bytes 5898240 | tf_op jit(solution)/shard_map/convert_element_type | solution.py:472
  193.1 2.7 %convert_reduce_fusion = f32[96,768]{1,0:T(8,128)} fusion(bf16[16,96,768]{2,1,0:T(8,128)(2,1)} %all-to-all-done.2), kind=kLoop, calls=%fused_computation.1 | loop fusion | flops 2285568 | bytes 2654208 | tf_op jit(solution)/shard_map/reduce_sum | solution.py:473
  (29 shorter events, 0.1 us)
Async XLA Ops:
  5.3 11.8 %copy-start.12 = (s32[192]{0:T(256)S(1)}, s32[192]{0:T(256)}, u32[]{:S(2)}) copy-start(s32[192]{0:T(256)} %param.9) | copy-start | bytes 2308
  5.3 52.7 %all-to-all-start = ((bf16[32,3,48,384]{3,2,1,0:T(8,128)(2,1)}), bf16[32,3,48,384]{3,2,1,0:T(8,128)(2,1)S(1)}, u32[]{:S(2)}, u32[]{:S(2)}) async-start(bf16[32,3,48,384]{3,2,1,0:T(8,128)(2,1)} %bitcast.34), calls=%async_computation | async-start | bytes 7077888 | tf_op jit(solution)/shard_map/all_to_all | solution.py:422
  13.0 48.6 %collective-permute-start.5 = (bf16[192,3072]{1,0:T(8,128)(2,1)}, bf16[192,3072]{1,0:T(8,128)(2,1)}, u32[]{:S(2)}, u32[]{:S(2)}) collective-permute-start(bf16[192,3072]{1,0:T(8,128)(2,1)} %refs_0_.1), channel_id=1, source_target_pairs={{0,3},{1,0},{2,1},{3,2},{4,7},{5,4},{6,5},{7,6},{8,11},{9,8},{10,9... | collective-permute-start | bytes 3538952 | tf_op jit(solution)/shard_map/ppermute | solution.py:417
  17.1 44.5 %collective-permute-start.4 = (bf16[192,3072]{1,0:T(8,128)(2,1)}, bf16[192,3072]{1,0:T(8,128)(2,1)}, u32[]{:S(2)}, u32[]{:S(2)}) collective-permute-start(bf16[192,3072]{1,0:T(8,128)(2,1)} %refs_0_.1), channel_id=1, source_target_pairs={{0,1},{1,2},{2,3},{3,0},{4,5},{5,6},{6,7},{7,4},{8,9},{9,10},{10,1... | collective-permute-start | bytes 3538952 | tf_op jit(solution)/shard_map/ppermute | solution.py:417
  17.1 6.1 %collective-permute-start = (s32[6,128]{1,0:T(8,128)}, s32[6,128]{1,0:T(8,128)}, u32[]{:S(2)}, u32[]{:S(2)}) collective-permute-start(s32[6,128]{1,0:T(8,128)} %bitcast.6), channel_id=1, source_target_pairs={{0,4},{4,0},{1,5},{5,1},{2,6},{6,2},{3,7},{7,3},{8,12},{12,8},{9,1... | collective-permute-start | bytes 9224 | tf_op jit(solution)/shard_map/ppermute | solution.py:384
  17.2 1.3 copy-start.8
  23.9 28.8 %collective-permute-start.2 = (s32[2,6,128]{2,1,0:T(8,128)S(1)}, s32[2,6,128]{2,1,0:T(8,128)S(1)}, u32[]{:S(2)}, u32[]{:S(2)}) collective-permute-start(s32[2,6,128]{2,1,0:T(8,128)S(1)} %get-tuple-element.68), channel_id=1, source_target_pairs={{0,16},{8,24},{16,0},{24,8},{1,17},{9,25},{17,1},{25,9},{2,18},{10... | collective-permute-start | bytes 18440 | tf_op jit(solution)/shard_map/ppermute | solution.py:384
  26.0 27.0 %collective-permute-start.1 = (s32[2,6,128]{2,1,0:T(8,128)S(1)}, s32[2,6,128]{2,1,0:T(8,128)S(1)}, u32[]{:S(2)}, u32[]{:S(2)}) collective-permute-start(s32[2,6,128]{2,1,0:T(8,128)S(1)} %get-tuple-element.68), channel_id=1, source_target_pairs={{0,8},{8,16},{16,24},{24,0},{1,9},{9,17},{17,25},{25,1},{2,10},{10... | collective-permute-start | bytes 18440 | tf_op jit(solution)/shard_map/ppermute | solution.py:384
  26.0 27.0 %collective-permute-start.3 = (s32[2,6,128]{2,1,0:T(8,128)S(1)}, s32[2,6,128]{2,1,0:T(8,128)S(1)}, u32[]{:S(2)}, u32[]{:S(2)}) collective-permute-start(s32[2,6,128]{2,1,0:T(8,128)S(1)} %get-tuple-element.68), channel_id=1, source_target_pairs={{0,24},{8,0},{16,8},{24,16},{1,25},{9,1},{17,9},{25,17},{2,26},{10... | collective-permute-start | bytes 18440 | tf_op jit(solution)/shard_map/ppermute | solution.py:384
  61.6 6.3 %copy-start.5 = (bf16[192,3072]{1,0:T(8,128)(2,1)S(1)}, bf16[192,3072]{1,0:T(8,128)(2,1)}, u32[]{:S(2)}) copy-start(bf16[192,3072]{1,0:T(8,128)(2,1)} %refs_0_.1) | copy-start | bytes 3538948
  61.6 10.2 %copy-start.9 = (s32[192]{0:T(256)S(1)}, s32[192]{0:T(256)}, u32[]{:S(2)}) copy-start(s32[192]{0:T(256)} %copy-done.8) | copy-start | bytes 2308
  61.6 10.5 %copy-start.7 = (s32[48,128]{1,0:T(8,128)S(1)}, s32[48,128]{1,0:T(8,128)}, u32[]{:S(2)}) copy-start(s32[48,128]{1,0:T(8,128)} %reshape.240) | copy-start | bytes 73732
  61.7 16.4 %copy-start.10 = (f32[768]{0:T(1024)S(1)}, f32[768]{0:T(1024)}, u32[]{:S(2)}) copy-start(f32[768]{0:T(1024)} %param.10) | copy-start | bytes 9220
  61.7 16.4 %copy-start.11 = (f32[768]{0:T(1024)S(1)}, f32[768]{0:T(1024)}, u32[]{:S(2)}) copy-start(f32[768]{0:T(1024)} %param.11) | copy-start | bytes 9220
  61.7 51.6 %all-to-all-start.1 = ((bf16[32,3,48,384]{3,2,1,0:T(8,128)(2,1)}), bf16[32,3,48,384]{3,2,1,0:T(8,128)(2,1)}, u32[]{:S(2)}, u32[]{:S(2)}) async-start(bf16[32,3,48,384]{3,2,1,0:T(8,128)(2,1)} %bitcast.4), calls=%async_computation.1 | async-start | bytes 7077888 | tf_op jit(solution)/shard_map/all_to_all | solution.py:429
  67.9 30.2 %collective-permute-start.6 = (bf16[192,3072]{1,0:T(8,128)(2,1)S(1)}, bf16[192,3072]{1,0:T(8,128)(2,1)S(1)}, u32[]{:S(2)}, u32[]{:S(2)}) collective-permute-start(bf16[192,3072]{1,0:T(8,128)(2,1)S(1)} %copy-done.5), channel_id=1, source_target_pairs={{0,2},{1,3},{2,0},{3,1},{4,6},{5,7},{6,4},{7,5},{8,10},{9,11},{10,... | collective-permute-start | bytes 3538952 | tf_op jit(solution)/shard_map/ppermute | solution.py:417
  72.4 36.3 %collective-permute-start.7 = (s32[6,128]{1,0:T(8,128)S(1)}, s32[6,128]{1,0:T(8,128)S(1)}, u32[]{:S(2)}, u32[]{:S(2)}) collective-permute-start(s32[6,128]{1,0:T(8,128)S(1)} %get-tuple-element.40), channel_id=1, source_target_pairs={{0,32},{32,64},{64,96},{96,0},{1,33},{33,65},{65,97},{97,1},{2,34}... | collective-permute-start | bytes 9224 | tf_op jit(solution)/shard_map/ppermute | solution.py:447
  73.9 39.1 %collective-permute-start.8 = (s32[6,128]{1,0:T(8,128)S(1)}, s32[6,128]{1,0:T(8,128)S(1)}, u32[]{:S(2)}, u32[]{:S(2)}) collective-permute-start(s32[6,128]{1,0:T(8,128)S(1)} %get-tuple-element.41), channel_id=1, source_target_pairs={{0,64},{32,96},{64,0},{96,32},{1,65},{33,97},{65,1},{97,33},{2,66}... | collective-permute-start | bytes 9224 | tf_op jit(solution)/shard_map/ppermute | solution.py:447
  76.6 36.4 %collective-permute-start.9 = (s32[6,128]{1,0:T(8,128)S(1)}, s32[6,128]{1,0:T(8,128)S(1)}, u32[]{:S(2)}, u32[]{:S(2)}) collective-permute-start(s32[6,128]{1,0:T(8,128)S(1)} %get-tuple-element.42), channel_id=1, source_target_pairs={{0,96},{32,0},{64,32},{96,64},{1,97},{33,1},{65,33},{97,65},{2,98}... | collective-permute-start | bytes 9224 | tf_op jit(solution)/shard_map/ppermute | solution.py:447
  78.1 35.2 %copy-start = (f32[1,768]{1,0:T(1,128)}, f32[1,768]{1,0:T(1,128)S(1)}, u32[]{:S(2)}) copy-start(f32[1,768]{1,0:T(1,128)S(1)} %broadcast_in_dim.84.qg_ref) | copy-start | bytes 9220
  78.1 35.2 %copy-start.1 = (f32[1,768]{1,0:T(1,128)}, f32[1,768]{1,0:T(1,128)S(1)}, u32[]{:S(2)}) copy-start(f32[1,768]{1,0:T(1,128)S(1)} %broadcast_in_dim.85.kg_ref) | copy-start | bytes 9220
  98.1 1.0 copy-start.6
  113.3 23.5 %copy-start.2 = (bf16[3072,768]{1,0:T(8,128)(2,1)S(1)}, bf16[3072,768]{1,0:T(8,128)(2,1)}, u32[]{:S(2)}) copy-start(bf16[3072,768]{1,0:T(8,128)(2,1)} %get-tuple-element.45) | copy-start | bytes 14155780
  132.4 9.1 %copy-start.3 = (bf16[768,768]{1,0:T(8,128)(2,1)}, bf16[768,768]{1,0:T(8,128)(2,1)S(1)}, u32[]{:S(2)}) copy-start(bf16[768,768]{1,0:T(8,128)(2,1)S(1)} %get-tuple-element.54.att_ref) | copy-start | bytes 3538948
  132.4 39.7 %collective-permute-start.10 = (bf16[192,3072]{1,0:T(8,128)(2,1)}, bf16[192,3072]{1,0:T(8,128)(2,1)}, u32[]{:S(2)}, u32[]{:S(2)}) collective-permute-start(bf16[192,3072]{1,0:T(8,128)(2,1)} %get-tuple-element.44), channel_id=1, source_target_pairs={{0,1},{1,2},{2,3},{3,0},{4,5},{5,6},{6,7},{7,4},{8,9},{9,10},{10,1... | collective-permute-start | bytes 3538952 | tf_op jit(solution)/shard_map/ppermute | solution.py:459
  134.6 53.0 %collective-permute-start.13 = (bf16[192,3072]{1,0:T(8,128)(2,1)}, bf16[192,3072]{1,0:T(8,128)(2,1)}, u32[]{:S(2)}, u32[]{:S(2)}) collective-permute-start(bf16[192,3072]{1,0:T(8,128)(2,1)} %get-tuple-element.49), channel_id=1, source_target_pairs={{0,3},{1,0},{2,1},{3,2},{4,7},{5,4},{6,5},{7,6},{8,11},{9,8},{10,9... | collective-permute-start | bytes 3538952 | tf_op jit(solution)/shard_map/ppermute | solution.py:459
  136.8 1.3 copy-start.4
  141.4 4.9 %collective-permute-start.11 = (bf16[16,96,768]{2,1,0:T(8,128)(2,1)}, bf16[16,96,768]{2,1,0:T(8,128)(2,1)}, u32[]{:S(2)}, u32[]{:S(2)}) collective-permute-start(bf16[16,96,768]{2,1,0:T(8,128)(2,1)} %weight_terms.3), channel_id=1, source_target_pairs={{0,4},{4,0},{1,5},{5,1},{2,6},{6,2},{3,7},{7,3},{8,12},{12,8},{9,1... | collective-permute-start | bytes 7077896 | tf_op jit(solution)/shard_map/ppermute | solution.py:463
  150.1 42.9 %all-to-all-start.2 = ((bf16[16,96,768]{2,1,0:T(8,128)(2,1)}), bf16[16,96,768]{2,1,0:T(8,128)(2,1)}, u32[]{:S(2)}, u32[]{:S(2)}) async-start(bf16[16,96,768]{2,1,0:T(8,128)(2,1)} %add_convert_fusion), calls=%async_computation.2 | async-start | bytes 4718592 | tf_op jit(solution)/shard_map/all_to_all | solution.py:469
  156.0 33.3 %collective-permute-start.12 = (bf16[192,3072]{1,0:T(8,128)(2,1)}, bf16[192,3072]{1,0:T(8,128)(2,1)}, u32[]{:S(2)}, u32[]{:S(2)}) collective-permute-start(bf16[192,3072]{1,0:T(8,128)(2,1)} %get-tuple-element.48), channel_id=1, source_target_pairs={{0,2},{1,3},{2,0},{3,1},{4,6},{5,7},{6,4},{7,5},{8,10},{9,11},{10,... | collective-permute-start | bytes 3538952 | tf_op jit(solution)/shard_map/ppermute | solution.py:467

commit v3 on v2

--- a/solution.py
+++ b/solution.py
@@ -175,7 +175,7 @@
     rows, heads = cuts * span, 2 * half // HD
     groups, width = heads // FORWARD_HEADS, FORWARD_HEADS * HD
     d_out = out_weight.shape[0]
-    blocks = 4
+    blocks = 3
     share = rows // places
     gain_spec = pl.BlockSpec((1, width), lambda step, here: (0, jnp.minimum(step, groups - 1)))
 

time: 197 us -> 196 us (level)
  no operation moved by 1% of the time
where the time goes in v3:
time: 196 us
  waiting for transfers between devices  72.4 us (37%)
  Pallas kernels  52.9 us (27%)
  starting transfers between devices  43.7 us (22%)
  other arithmetic  14.3 us (7%)
  local copies, waits for them, and re-layouts  11.4 us (6%)
    ppermute x4, waiting for transfers between devices, gathered(): lax.ppermute(own, axis, turn(size, by))  25 us
    ppermute x3, waiting for transfers between devices, body(): lax.ppermute(cotangent, 'mp', turn(places, by))  20 us
    pallas_call x1, Pallas kernels, attention_forward(): pl.pallas_call(functools.partial(forward_kernel, groups), grid_spec=pltpu...  18.8 us
    ppermute x2, waiting for transfers between devices, body(): partials[by] = lax.ppermute(partials[by], 'mp', turn(places, by))  15.4 us
    pallas_call x1, Pallas kernels, attention_backward(): pl.pallas_call(functools.partial(backward_kernel, BACKWARD_ROWS), grid=(h...  14.3 us
    pallas_call x1, Pallas kernels, grad_products(): pl.pallas_call(grad_kernel, grid_spec=pltpu.PrefetchScalarGridSpec(num_sc...  9.31 us
    ppermute x3, starting transfers between devices, body(): lax.ppermute(cotangent, 'mp', turn(places, by))  8.06 us
    all_to_all x1, starting transfers between devices, body(): spread = lax.all_to_all(pieces, DP, split_axis=0, concat_axis=0, tiled=True)  7.67 us
  transfers between devices with their start and end apart: 17, of which 9 were waited for; matrix products, arithmetic and copies ran while one was open for 11% of the time, Pallas kernels for 15%

profile of v3, /device:TPU:8, one launch (start us, length us, event | category | flops | bytes accessed | tf_op | source)
XLA Modules:
  0.0 195.6 jit_solution(14461668043852170523)
XLA Ops:
  0.6 4.7 %cut_blocks.1 = bf16[16,2,3,48,384]{4,3,2,1,0:T(8,128)(2,1)} custom-call(bf16[3,768,768]{2,1,0:T(8,128)(2,1)} %bitcast.35), custom_call_target="tpu_custom_call" | custom-call | bytes 7077888 | tf_op jit(solution)/shard_map/cut_blocks/pallas_call | solution.py:271
  5.3 7.7 %all-to-all-start = ((bf16[32,3,48,384]{3,2,1,0:T(8,128)(2,1)}), bf16[32,3,48,384]{3,2,1,0:T(8,128)(2,1)S(1)}, u32[]{:S(2)}, u32[]{:S(2)}) async-start(bf16[32,3,48,384]{3,2,1,0:T(8,128)(2,1)} %bitcast.34), calls=%async_computation | async-start | bytes 7077888 | tf_op jit(solution)/shard_map/all_to_all | solution.py:422
  13.0 4.1 %collective-permute-start.5 = (bf16[192,3072]{1,0:T(8,128)(2,1)}, bf16[192,3072]{1,0:T(8,128)(2,1)}, u32[]{:S(2)}, u32[]{:S(2)}) collective-permute-start(bf16[192,3072]{1,0:T(8,128)(2,1)} %refs_0_.1), channel_id=1, source_target_pairs={{0,3},{1,0},{2,1},{3,2},{4,7},{5,4},{6,5},{7,6},{8,11},{9,8},{10,9... | collective-permute-start | bytes 3538952 | tf_op jit(solution)/shard_map/ppermute | solution.py:417
  17.1 0.0 collective-permute-start.4
  17.1 0.0 collective-permute-start
  17.1 0.1 select_reduce_fusion
  17.3 0.7 ne.200
  18.0 0.6 broadcast_divide_fusion
  18.6 0.8 div.99
  19.4 1.4 rem.317
  20.7 0.7 fusion
  21.5 0.7 add_add_fusion
  22.2 1.0 reshape.247
  23.2 0.7 fusion.21
  23.9 2.1 %collective-permute-start.2 = (s32[2,6,128]{2,1,0:T(8,128)S(1)}, s32[2,6,128]{2,1,0:T(8,128)S(1)}, u32[]{:S(2)}, u32[]{:S(2)}) collective-permute-start(s32[2,6,128]{2,1,0:T(8,128)S(1)} %get-tuple-element.68), channel_id=1, source_target_pairs={{0,16},{8,24},{16,0},{24,8},{1,17},{9,25},{17,1},{25,9},{2,18},{10... | collective-permute-start | bytes 18440 | tf_op jit(solution)/shard_map/ppermute | solution.py:384
  26.0 0.0 collective-permute-start.1
  26.0 2.0 %collective-permute-start.3 = (s32[2,6,128]{2,1,0:T(8,128)S(1)}, s32[2,6,128]{2,1,0:T(8,128)S(1)}, u32[]{:S(2)}, u32[]{:S(2)}) collective-permute-start(s32[2,6,128]{2,1,0:T(8,128)S(1)} %get-tuple-element.68), channel_id=1, source_target_pairs={{0,24},{8,0},{16,8},{24,16},{1,25},{9,1},{17,9},{25,17},{2,26},{10... | collective-permute-start | bytes 18440 | tf_op jit(solution)/shard_map/ppermute | solution.py:384
  28.0 24.7 %collective-permute-done.2 = s32[2,6,128]{2,1,0:T(8,128)S(1)} collective-permute-done((s32[2,6,128]{2,1,0:T(8,128)S(1)}, s32[2,6,128]{2,1,0:T(8,128)S(1)}, u32[]{:S(2)}, u32[]{:S(2)}) %collective-permute-start.2) | collective-permute-done | bytes 6176 | tf_op jit(solution)/shard_map/ppermute | solution.py:384
  52.7 0.3 collective-permute-done.1
  53.0 0.0 collective-permute-done.3
  53.0 0.6 pad_add_fusion
  53.6 1.4 reshape.240
  54.9 3.1 %all-to-all-done = bf16[32,3,48,384]{3,2,1,0:T(8,128)(2,1)S(1)} async-done(((bf16[32,3,48,384]{3,2,1,0:T(8,128)(2,1)}), bf16[32,3,48,384]{3,2,1,0:T(8,128)(2,1)S(1)}, u32[]{:S(2)}, u32[]{:S(2)}) %all-to-all-start) | async-done | bytes 3538976 | tf_op jit(solution)/shard_map/all_to_all | solution.py:422
  58.0 3.6 %gather_fusion = bf16[576,8,384]{2,1,0:T(8,128)(2,1)} fusion(bf16[576,8,384]{2,1,0:T(8,128)(2,1)S(1)} %bitcast.33, s32[1024]{0:T(1024)S(1)} %pad_clamp_fusion), kind=kCustom, calls=%fused_computation | custom fusion | bytes 7080192 | tf_op jit(solution)/shard_map/jit(_take)/gather | solution.py:423
  61.6 0.0 collective-permute-done.5.refs_3_
  61.6 0.0 collective-permute-done.4.refs_1_
  61.6 0.0 copy-start.7
  61.7 0.0 copy-start.10
  61.7 0.0 copy-start.11
  61.7 6.2 %all-to-all-start.1 = ((bf16[32,3,48,384]{3,2,1,0:T(8,128)(2,1)}), bf16[32,3,48,384]{3,2,1,0:T(8,128)(2,1)}, u32[]{:S(2)}, u32[]{:S(2)}) async-start(bf16[32,3,48,384]{3,2,1,0:T(8,128)(2,1)} %bitcast.4), calls=%async_computation.1 | async-start | bytes 7077888 | tf_op jit(solution)/shard_map/all_to_all | solution.py:429
  67.9 4.0 %collective-permute-start.6 = (bf16[192,3072]{1,0:T(8,128)(2,1)S(1)}, bf16[192,3072]{1,0:T(8,128)(2,1)S(1)}, u32[]{:S(2)}, u32[]{:S(2)}) collective-permute-start(bf16[192,3072]{1,0:T(8,128)(2,1)S(1)} %copy-done.5), channel_id=1, source_target_pairs={{0,2},{1,3},{2,0},{3,1},{4,6},{5,7},{6,4},{7,5},{8,10},{9,11},{10,... | collective-permute-start | bytes 3538952 | tf_op jit(solution)/shard_map/ppermute | solution.py:417
  71.8 0.1 compare_select_fusion.19
  72.0 0.1 iota_compare_fusion.3
  72.1 0.1 iota_compare_fusion.1
  72.1 0.2 select_reduce_fusion.1
  72.4 1.5 collective-permute-start.7
  73.9 2.7 %collective-permute-start.8 = (s32[6,128]{1,0:T(8,128)S(1)}, s32[6,128]{1,0:T(8,128)S(1)}, u32[]{:S(2)}, u32[]{:S(2)}) collective-permute-start(s32[6,128]{1,0:T(8,128)S(1)} %get-tuple-element.41), channel_id=1, source_target_pairs={{0,64},{32,96},{64,0},{96,32},{1,65},{33,97},{65,1},{97,33},{2,66}... | collective-permute-start | bytes 9224 | tf_op jit(solution)/shard_map/ppermute | solution.py:447
  76.6 1.4 collective-permute-start.9
  78.1 0.0 copy-start
  78.1 20.0 %collective-permute-done.6.refs_2_ = bf16[192,3072]{1,0:T(8,128)(2,1)S(1)} collective-permute-done((bf16[192,3072]{1,0:T(8,128)(2,1)S(1)}, bf16[192,3072]{1,0:T(8,128)(2,1)S(1)}, u32[]{:S(2)}, u32[]{:S(2)}) %collective-permute-start.6) | collective-permute-done | bytes 1179680 | tf_op jit(solution)/shard_map/ppermute | solution.py:417
  98.1 1.0 copy-done.6
  99.1 9.3 %grad_products.1 = (bf16[768,768]{1,0:T(8,128)(2,1)}, bf16[3072,768]{1,0:T(8,128)(2,1)}) custom-call(s32[1]{0:T(128)} %bitcast.here_ref, bf16[192,3072]{1,0:T(8,128)(2,1)} %refs_0_.1, bf16[192,3072]{1,0:T(8,128)(2,1)} %collective-permute-done.4.refs_1_, bf16[192,3072]{1,0:T(8,128)(2,1)} %copy-done.6, bf16[192,3072]{1,0:T(8,128)(2,1)} %collective-permute-done.5.refs_3_, ...), custom_call_target="tpu_custom_call" | custom-call | flops 1 | bytes 1 | tf_op jit(solution)/shard_map/grad_products/pallas_call | solution.py:317
  108.4 0.3 collective-permute-done.7
  108.7 4.3 %collective-permute-done.8 = s32[6,128]{1,0:T(8,128)S(1)} collective-permute-done((s32[6,128]{1,0:T(8,128)S(1)}, s32[6,128]{1,0:T(8,128)S(1)}, u32[]{:S(2)}, u32[]{:S(2)}) %collective-permute-start.8) | collective-permute-done | bytes 3104 | tf_op jit(solution)/shard_map/ppermute | solution.py:447
  113.0 0.0 collective-permute-done.9
  113.0 0.2 copy.13
  113.2 0.0 all-to-all-done.1
  113.3 18.8 %attention_forward.1 = (bf16[768,768]{1,0:T(8,128)(2,1)S(1)}, bf16[6,768,768]{2,1,0:T(8,128)(2,1)}, bf16[192,3072]{1,0:T(8,128)(2,1)S(1)}, bf16[192,3072]{1,0:T(...) custom-call(s32[1]{0:T(128)} %bitcast.here_ref, ...), custom_call_target="tpu_custom_call" | custom-call | flops 5435817984 | bytes 21233664 | tf_op jit(solution)/shard_map/attention_forward/pallas_call | solution.py:185
  132.1 2.2 %collective-permute-start.10 = (bf16[192,3072]{1,0:T(8,128)(2,1)}, bf16[192,3072]{1,0:T(8,128)(2,1)}, u32[]{:S(2)}, u32[]{:S(2)}) collective-permute-start(bf16[192,3072]{1,0:T(8,128)(2,1)} %get-tuple-element.44), channel_id=1, source_target_pairs={{0,1},{1,2},{2,3},{3,0},{4,5},{5,6},{6,7},{7,4},{8,9},{9,10},{10,1... | collective-permute-start | bytes 3538952 | tf_op jit(solution)/shard_map/ppermute | solution.py:459
  134.3 2.2 %collective-permute-start.13 = (bf16[192,3072]{1,0:T(8,128)(2,1)}, bf16[192,3072]{1,0:T(8,128)(2,1)}, u32[]{:S(2)}, u32[]{:S(2)}) collective-permute-start(bf16[192,3072]{1,0:T(8,128)(2,1)} %get-tuple-element.49), channel_id=1, source_target_pairs={{0,3},{1,0},{2,1},{3,2},{4,7},{5,4},{6,5},{7,6},{8,11},{9,8},{10,9... | collective-permute-start | bytes 3538952 | tf_op jit(solution)/shard_map/ppermute | solution.py:459
  136.5 1.3 copy-done.4
  137.8 3.4 %weight_terms.3 = bf16[16,96,768]{2,1,0:T(8,128)(2,1)} custom-call(s32[1]{0:T(128)} %bitcast.15.core_ref, bf16[16,2,96,768]{3,2,1,0:T(8,128)(2,1)S(1)} %bitcast.31, bf16[768,768]{1,0:T(8,128)(2,1)S(1)} %copy-done.4), custom_call_target="tpu_custom_call" | custom-call | flops 999999995904 | bytes 1000000000 | tf_op jit(solution)/shard_map/weight_terms/pallas_call | solution.py:356
  141.2 0.0 collective-permute-start.11
  141.2 2.4 %weight_terms.2 = bf16[16,96,768]{2,1,0:T(8,128)(2,1)S(1)} custom-call(s32[1]{0:T(128)} %bitcast.13.core_ref, bf16[16,2,96,768]{3,2,1,0:T(8,128)(2,1)S(1)} %bitcast.32, bf16[768,768]{1,0:T(8,128)(2,1)S(1)} %copy-done.4), custom_call_target="tpu_custom_call" | custom-call | flops 999999995904 | bytes 1000000000 | tf_op jit(solution)/shard_map/weight_terms/pallas_call | solution.py:356
  143.6 2.5 %collective-permute-done.11 = bf16[16,96,768]{2,1,0:T(8,128)(2,1)} collective-permute-done((bf16[16,96,768]{2,1,0:T(8,128)(2,1)}, bf16[16,96,768]{2,1,0:T(8,128)(2,1)}, u32[]{:S(2)}, u32[]{:S(2)}) %collective-permute-start.11) | collective-permute-done | bytes 2359328 | tf_op jit(solution)/shard_map/ppermute | solution.py:463
  146.1 3.8 %add_convert_fusion = bf16[16,96,768]{2,1,0:T(8,128)(2,1)} fusion(bf16[16,96,768]{2,1,0:T(8,128)(2,1)} %collective-permute-done.11, bf16[16,96,768]{2,1,0:T(8,128)(2,1)S(1)} %weight_terms.2), kind=kLoop, calls=%fused_computation.2 | loop fusion | flops 4718592 | bytes 7077888 | tf_op jit(solution)/shard_map/convert_element_type | solution.py:465
  149.9 5.9 %all-to-all-start.2 = ((bf16[16,96,768]{2,1,0:T(8,128)(2,1)}), bf16[16,96,768]{2,1,0:T(8,128)(2,1)}, u32[]{:S(2)}, u32[]{:S(2)}) async-start(bf16[16,96,768]{2,1,0:T(8,128)(2,1)} %add_convert_fusion), calls=%async_computation.2 | async-start | bytes 4718592 | tf_op jit(solution)/shard_map/all_to_all | solution.py:469
  155.8 1.8 collective-permute-start.12
  157.5 14.3 %attention_backward.1 = bf16[3,768,768]{2,1,0:T(8,128)(2,1)} custom-call(bf16[16,2,3,48,384]{4,3,2,1,0:T(8,128)(2,1)} %bitcast.12.q_ref.k_ref.v_ref, bf16[16,2,3,48,384]{4,3,2,1,0:T(8,128)(2,1)} %bitcast.12.q_ref.k_ref.v_ref, bf16[16,2,3,48,384]{4,3,2,1,0:T(8,128)(2,1)} %bitcast.12.q_ref.k_ref.v_ref, bf16[6,768,768]{2,1,0:T(8,128)(2,1)} %get-tuple-element.52.prob_ref, ...), custom_call_target="tpu_custom_call" | custom-call | flops 999999995904 | bytes 1000000000 | tf_op jit(solution)/shard_map/attention_backward/pallas_call | solution.py:239
  171.8 0.0 collective-permute-done.10
  171.8 15.4 %collective-permute-done.13 = bf16[192,3072]{1,0:T(8,128)(2,1)} collective-permute-done((bf16[192,3072]{1,0:T(8,128)(2,1)}, bf16[192,3072]{1,0:T(8,128)(2,1)}, u32[]{:S(2)}, u32[]{:S(2)}) %collective-permute-start.13) | collective-permute-done | bytes 1179680 | tf_op jit(solution)/shard_map/ppermute | solution.py:459
  187.3 1.8 collective-permute-done.12
  189.1 3.7 %add_convert_fusion.1 = bf16[192,3072]{1,0:T(8,128)(2,1)} fusion(bf16[192,3072]{1,0:T(8,128)(2,1)} %collective-permute-done.13, bf16[192,3072]{1,0:T(8,128)(2,1)} %collective-permute-done.12, bf16[192,3072]{1,0:T(8,128)(2,1)} %collective-permute-done.10, bf16[192,3072]{1,0:T(8,128)(2,1)S(1)} %get-tuple-element.55), kind=kLoop, calls=%fused_computation.3 | loop fusion | flops 4718592 | bytes 5898240 | tf_op jit(solution)/shard_map/convert_element_type | solution.py:472
  192.8 2.7 %convert_reduce_fusion = f32[96,768]{1,0:T(8,128)} fusion(bf16[16,96,768]{2,1,0:T(8,128)(2,1)} %all-to-all-done.2), kind=kLoop, calls=%fused_computation.1 | loop fusion | flops 2285568 | bytes 2654208 | tf_op jit(solution)/shard_map/reduce_sum | solution.py:473
  (29 shorter events, 0.1 us)
Async XLA Ops:
  5.3 11.8 %copy-start.12 = (s32[192]{0:T(256)S(1)}, s32[192]{0:T(256)}, u32[]{:S(2)}) copy-start(s32[192]{0:T(256)} %param.9) | copy-start | bytes 2308
  5.3 52.7 %all-to-all-start = ((bf16[32,3,48,384]{3,2,1,0:T(8,128)(2,1)}), bf16[32,3,48,384]{3,2,1,0:T(8,128)(2,1)S(1)}, u32[]{:S(2)}, u32[]{:S(2)}) async-start(bf16[32,3,48,384]{3,2,1,0:T(8,128)(2,1)} %bitcast.34), calls=%async_computation | async-start | bytes 7077888 | tf_op jit(solution)/shard_map/all_to_all | solution.py:422
  13.0 48.6 %collective-permute-start.5 = (bf16[192,3072]{1,0:T(8,128)(2,1)}, bf16[192,3072]{1,0:T(8,128)(2,1)}, u32[]{:S(2)}, u32[]{:S(2)}) collective-permute-start(bf16[192,3072]{1,0:T(8,128)(2,1)} %refs_0_.1), channel_id=1, source_target_pairs={{0,3},{1,0},{2,1},{3,2},{4,7},{5,4},{6,5},{7,6},{8,11},{9,8},{10,9... | collective-permute-start | bytes 3538952 | tf_op jit(solution)/shard_map/ppermute | solution.py:417
  17.1 44.5 %collective-permute-start.4 = (bf16[192,3072]{1,0:T(8,128)(2,1)}, bf16[192,3072]{1,0:T(8,128)(2,1)}, u32[]{:S(2)}, u32[]{:S(2)}) collective-permute-start(bf16[192,3072]{1,0:T(8,128)(2,1)} %refs_0_.1), channel_id=1, source_target_pairs={{0,1},{1,2},{2,3},{3,0},{4,5},{5,6},{6,7},{7,4},{8,9},{9,10},{10,1... | collective-permute-start | bytes 3538952 | tf_op jit(solution)/shard_map/ppermute | solution.py:417
  17.1 6.1 %collective-permute-start = (s32[6,128]{1,0:T(8,128)}, s32[6,128]{1,0:T(8,128)}, u32[]{:S(2)}, u32[]{:S(2)}) collective-permute-start(s32[6,128]{1,0:T(8,128)} %bitcast.6), channel_id=1, source_target_pairs={{0,4},{4,0},{1,5},{5,1},{2,6},{6,2},{3,7},{7,3},{8,12},{12,8},{9,1... | collective-permute-start | bytes 9224 | tf_op jit(solution)/shard_map/ppermute | solution.py:384
  17.2 1.3 copy-start.8
  23.9 28.8 %collective-permute-start.2 = (s32[2,6,128]{2,1,0:T(8,128)S(1)}, s32[2,6,128]{2,1,0:T(8,128)S(1)}, u32[]{:S(2)}, u32[]{:S(2)}) collective-permute-start(s32[2,6,128]{2,1,0:T(8,128)S(1)} %get-tuple-element.68), channel_id=1, source_target_pairs={{0,16},{8,24},{16,0},{24,8},{1,17},{9,25},{17,1},{25,9},{2,18},{10... | collective-permute-start | bytes 18440 | tf_op jit(solution)/shard_map/ppermute | solution.py:384
  26.0 27.0 %collective-permute-start.1 = (s32[2,6,128]{2,1,0:T(8,128)S(1)}, s32[2,6,128]{2,1,0:T(8,128)S(1)}, u32[]{:S(2)}, u32[]{:S(2)}) collective-permute-start(s32[2,6,128]{2,1,0:T(8,128)S(1)} %get-tuple-element.68), channel_id=1, source_target_pairs={{0,8},{8,16},{16,24},{24,0},{1,9},{9,17},{17,25},{25,1},{2,10},{10... | collective-permute-start | bytes 18440 | tf_op jit(solution)/shard_map/ppermute | solution.py:384
  26.0 27.0 %collective-permute-start.3 = (s32[2,6,128]{2,1,0:T(8,128)S(1)}, s32[2,6,128]{2,1,0:T(8,128)S(1)}, u32[]{:S(2)}, u32[]{:S(2)}) collective-permute-start(s32[2,6,128]{2,1,0:T(8,128)S(1)} %get-tuple-element.68), channel_id=1, source_target_pairs={{0,24},{8,0},{16,8},{24,16},{1,25},{9,1},{17,9},{25,17},{2,26},{10... | collective-permute-start | bytes 18440 | tf_op jit(solution)/shard_map/ppermute | solution.py:384
  61.6 6.3 %copy-start.5 = (bf16[192,3072]{1,0:T(8,128)(2,1)S(1)}, bf16[192,3072]{1,0:T(8,128)(2,1)}, u32[]{:S(2)}) copy-start(bf16[192,3072]{1,0:T(8,128)(2,1)} %refs_0_.1) | copy-start | bytes 3538948
  61.6 10.2 %copy-start.9 = (s32[192]{0:T(256)S(1)}, s32[192]{0:T(256)}, u32[]{:S(2)}) copy-start(s32[192]{0:T(256)} %copy-done.8) | copy-start | bytes 2308
  61.6 10.5 %copy-start.7 = (s32[48,128]{1,0:T(8,128)S(1)}, s32[48,128]{1,0:T(8,128)}, u32[]{:S(2)}) copy-start(s32[48,128]{1,0:T(8,128)} %reshape.240) | copy-start | bytes 73732
  61.7 16.4 %copy-start.10 = (f32[768]{0:T(1024)S(1)}, f32[768]{0:T(1024)}, u32[]{:S(2)}) copy-start(f32[768]{0:T(1024)} %param.10) | copy-start | bytes 9220
  61.7 16.4 %copy-start.11 = (f32[768]{0:T(1024)S(1)}, f32[768]{0:T(1024)}, u32[]{:S(2)}) copy-start(f32[768]{0:T(1024)} %param.11) | copy-start | bytes 9220
  61.7 51.6 %all-to-all-start.1 = ((bf16[32,3,48,384]{3,2,1,0:T(8,128)(2,1)}), bf16[32,3,48,384]{3,2,1,0:T(8,128)(2,1)}, u32[]{:S(2)}, u32[]{:S(2)}) async-start(bf16[32,3,48,384]{3,2,1,0:T(8,128)(2,1)} %bitcast.4), calls=%async_computation.1 | async-start | bytes 7077888 | tf_op jit(solution)/shard_map/all_to_all | solution.py:429
  67.9 30.2 %collective-permute-start.6 = (bf16[192,3072]{1,0:T(8,128)(2,1)S(1)}, bf16[192,3072]{1,0:T(8,128)(2,1)S(1)}, u32[]{:S(2)}, u32[]{:S(2)}) collective-permute-start(bf16[192,3072]{1,0:T(8,128)(2,1)S(1)} %copy-done.5), channel_id=1, source_target_pairs={{0,2},{1,3},{2,0},{3,1},{4,6},{5,7},{6,4},{7,5},{8,10},{9,11},{10,... | collective-permute-start | bytes 3538952 | tf_op jit(solution)/shard_map/ppermute | solution.py:417
  72.4 36.3 %collective-permute-start.7 = (s32[6,128]{1,0:T(8,128)S(1)}, s32[6,128]{1,0:T(8,128)S(1)}, u32[]{:S(2)}, u32[]{:S(2)}) collective-permute-start(s32[6,128]{1,0:T(8,128)S(1)} %get-tuple-element.40), channel_id=1, source_target_pairs={{0,32},{32,64},{64,96},{96,0},{1,33},{33,65},{65,97},{97,1},{2,34}... | collective-permute-start | bytes 9224 | tf_op jit(solution)/shard_map/ppermute | solution.py:447
  73.9 39.1 %collective-permute-start.8 = (s32[6,128]{1,0:T(8,128)S(1)}, s32[6,128]{1,0:T(8,128)S(1)}, u32[]{:S(2)}, u32[]{:S(2)}) collective-permute-start(s32[6,128]{1,0:T(8,128)S(1)} %get-tuple-element.41), channel_id=1, source_target_pairs={{0,64},{32,96},{64,0},{96,32},{1,65},{33,97},{65,1},{97,33},{2,66}... | collective-permute-start | bytes 9224 | tf_op jit(solution)/shard_map/ppermute | solution.py:447
  76.6 36.4 %collective-permute-start.9 = (s32[6,128]{1,0:T(8,128)S(1)}, s32[6,128]{1,0:T(8,128)S(1)}, u32[]{:S(2)}, u32[]{:S(2)}) collective-permute-start(s32[6,128]{1,0:T(8,128)S(1)} %get-tuple-element.42), channel_id=1, source_target_pairs={{0,96},{32,0},{64,32},{96,64},{1,97},{33,1},{65,33},{97,65},{2,98}... | collective-permute-start | bytes 9224 | tf_op jit(solution)/shard_map/ppermute | solution.py:447
  78.1 35.2 %copy-start = (f32[1,768]{1,0:T(1,128)}, f32[1,768]{1,0:T(1,128)S(1)}, u32[]{:S(2)}) copy-start(f32[1,768]{1,0:T(1,128)S(1)} %broadcast_in_dim.84.qg_ref) | copy-start | bytes 9220
  78.1 35.2 %copy-start.1 = (f32[1,768]{1,0:T(1,128)}, f32[1,768]{1,0:T(1,128)S(1)}, u32[]{:S(2)}) copy-start(f32[1,768]{1,0:T(1,128)S(1)} %broadcast_in_dim.85.kg_ref) | copy-start | bytes 9220
  98.1 1.0 copy-start.6
  113.3 23.3 %copy-start.2 = (bf16[3072,768]{1,0:T(8,128)(2,1)S(1)}, bf16[3072,768]{1,0:T(8,128)(2,1)}, u32[]{:S(2)}) copy-start(bf16[3072,768]{1,0:T(8,128)(2,1)} %get-tuple-element.45) | copy-start | bytes 14155780
  132.1 9.1 %copy-start.3 = (bf16[768,768]{1,0:T(8,128)(2,1)}, bf16[768,768]{1,0:T(8,128)(2,1)S(1)}, u32[]{:S(2)}) copy-start(bf16[768,768]{1,0:T(8,128)(2,1)S(1)} %get-tuple-element.54.att_ref) | copy-start | bytes 3538948
  132.1 39.7 %collective-permute-start.10 = (bf16[192,3072]{1,0:T(8,128)(2,1)}, bf16[192,3072]{1,0:T(8,128)(2,1)}, u32[]{:S(2)}, u32[]{:S(2)}) collective-permute-start(bf16[192,3072]{1,0:T(8,128)(2,1)} %get-tuple-element.44), channel_id=1, source_target_pairs={{0,1},{1,2},{2,3},{3,0},{4,5},{5,6},{6,7},{7,4},{8,9},{9,10},{10,1... | collective-permute-start | bytes 3538952 | tf_op jit(solution)/shard_map/ppermute | solution.py:459
  134.3 53.0 %collective-permute-start.13 = (bf16[192,3072]{1,0:T(8,128)(2,1)}, bf16[192,3072]{1,0:T(8,128)(2,1)}, u32[]{:S(2)}, u32[]{:S(2)}) collective-permute-start(bf16[192,3072]{1,0:T(8,128)(2,1)} %get-tuple-element.49), channel_id=1, source_target_pairs={{0,3},{1,0},{2,1},{3,2},{4,7},{5,4},{6,5},{7,6},{8,11},{9,8},{10,9... | collective-permute-start | bytes 3538952 | tf_op jit(solution)/shard_map/ppermute | solution.py:459
  136.5 1.3 copy-start.4
  141.2 4.9 %collective-permute-start.11 = (bf16[16,96,768]{2,1,0:T(8,128)(2,1)}, bf16[16,96,768]{2,1,0:T(8,128)(2,1)}, u32[]{:S(2)}, u32[]{:S(2)}) collective-permute-start(bf16[16,96,768]{2,1,0:T(8,128)(2,1)} %weight_terms.3), channel_id=1, source_target_pairs={{0,4},{4,0},{1,5},{5,1},{2,6},{6,2},{3,7},{7,3},{8,12},{12,8},{9,1... | collective-permute-start | bytes 7077896 | tf_op jit(solution)/shard_map/ppermute | solution.py:463
  149.9 42.9 %all-to-all-start.2 = ((bf16[16,96,768]{2,1,0:T(8,128)(2,1)}), bf16[16,96,768]{2,1,0:T(8,128)(2,1)}, u32[]{:S(2)}, u32[]{:S(2)}) async-start(bf16[16,96,768]{2,1,0:T(8,128)(2,1)} %add_convert_fusion), calls=%async_computation.2 | async-start | bytes 4718592 | tf_op jit(solution)/shard_map/all_to_all | solution.py:469
  155.8 33.3 %collective-permute-start.12 = (bf16[192,3072]{1,0:T(8,128)(2,1)}, bf16[192,3072]{1,0:T(8,128)(2,1)}, u32[]{:S(2)}, u32[]{:S(2)}) collective-permute-start(bf16[192,3072]{1,0:T(8,128)(2,1)} %get-tuple-element.48), channel_id=1, source_target_pairs={{0,2},{1,3},{2,0},{3,1},{4,6},{5,7},{6,4},{7,5},{8,10},{9,11},{10,... | collective-permute-start | bytes 3538952 | tf_op jit(solution)/shard_map/ppermute | solution.py:467
